TPU v7x, 32 devices: a whole 2x2x4 slice. The times are simulated.
32 devices in a mesh: parts: 2 (over x), wide: 16 (over z, y, core).
Axes of the slice: x: 2, y: 2, z: 4, core: 2. Of those that a mesh axis runs over, the one named last changes fastest.
Arguments:
- tokens: bfloat16 [1024, 8192], P('parts', 'wide'), parts along dimension 0, may hold values from -1100 to 1100
- norm_gain: float32 [8192], replicated, may hold values from 0.25 to 1.75
- gate_weight: bfloat16 [16, 2048, 8192], P('wide'), may hold values from -0.0625 to 0.0625
- up_weight: bfloat16 [16, 2048, 8192], P('wide'), may hold values from -0.0625 to 0.0625
- down_weight: bfloat16 [16, 8192, 2048], P('wide'), may hold values from -0.03125 to 0.03125
Outputs:
- layer_output: bfloat16 [1024, 8192], P('parts', 'wide'), parts along dimension 0
There are 2 independent parts, one for each index of `parts`. A program takes and returns all parts, laid end to end along the dimension named above; an argument that names none is the same for every part. Nothing has to cross between parts.
All inputs are finite; a program needn't handle non-finite values.
Results may differ from a plain program's by a relative error of at most 0.0065.
Values may be sent and summed in bfloat16 or wider, within the bound.
A program may use at most 256 MiB of HBM per device.

v0:
```python
import jax
import jax.numpy as jnp
from jax import lax
from jax.experimental import pallas as pl
from jax.experimental.pallas import tpu as pltpu
from jax.sharding import PartitionSpec as P

WSPLIT = 4
ROW_CHUNKS = 2
UNIT_CHUNKS = 4

epsilon = 1e-05


def partner(block, bit):
    count = lax.axis_size("wide")
    return lax.ppermute(block, "wide", [(i, i ^ (1 << bit)) for i in range(count)])


def shift(block, groups, step, valid):
    route = []
    for h in valid:
        if 0 <= h < groups and 0 <= h + step < groups:
            route += [
                (h * WSPLIT + lane, (h + step) * WSPLIT + lane) for lane in range(WSPLIT)
            ]
    return lax.ppermute(block, "wide", route)


def gather_groups(block, group, groups):
    rows, piece = block.shape
    pieces = jnp.zeros((groups, rows, piece), block.dtype)
    pieces = lax.dynamic_update_index_in_dim(pieces, block, group, 0)
    right = left = block
    for step in range(1, groups):
        right = shift(right, groups, 1, range(groups - 1))
        left = shift(left, groups, -1, range(1, groups))
        low, high = group - step, group + step
        index = lax.broadcasted_iota(jnp.int32, (groups, 1, 1), 0)
        pieces = jnp.where(index == low, right[None], pieces)
        pieces = jnp.where(index == high, left[None], pieces)
    return jnp.concatenate([pieces[h] for h in range(groups)], axis=1)


def scatter_groups(result, group, groups):
    rows, width = result.shape
    piece = width // groups

    def block(index):
        index = jnp.clip(index, 0, groups - 1)
        return lax.dynamic_slice(result, (0, index * piece), (rows, piece))

    last = groups - 1
    right = left = None
    for step in range(last):
        out_right = block(group + last - step)
        out_left = block(group - last + step)
        if right is not None:
            out_right = out_right + right.astype(jnp.float32)
            out_left = out_left + left.astype(jnp.float32)
        right = shift(out_right.astype(jnp.bfloat16), groups, 1, range(step + 1))
        left = shift(out_left.astype(jnp.bfloat16), groups, -1, range(last - step, groups))
    mine = block(group)
    if right is not None:
        mine = mine + right.astype(jnp.float32) + left.astype(jnp.float32)
    return mine.astype(jnp.bfloat16)


def product(a, weight):
    return jnp.dot(a, weight, preferred_element_type=jnp.float32)


def params(flops, bytes_accessed):
    return dict(
        compiler_params=pltpu.CompilerParams(vmem_limit_bytes=40 * 2**20),
        cost_estimate=pl.CostEstimate(
            flops=flops, bytes_accessed=bytes_accessed, transcendentals=0
        ),
    )


def away_kernel(order, a, gate, up, gate_out, up_out):
    gate_out[...] = product(a[...], gate[0]).astype(jnp.bfloat16)
    up_out[...] = product(a[...], up[0]).astype(jnp.bfloat16)


def project_away(a, gate, up, order, tile):
    m, k = a.shape
    n = order.shape[0]
    weight = pl.BlockSpec((1, k, tile), lambda j, order: (0, 0, order[j]))
    out = pl.BlockSpec((m, tile), lambda j, order: (0, j))
    return pl.pallas_call(
        away_kernel,
        grid_spec=pltpu.PrefetchScalarGridSpec(
            num_scalar_prefetch=1,
            grid=(n,),
            in_specs=[pl.BlockSpec((m, k), lambda j, order: (0, 0)), weight, weight],
            out_specs=[out, out],
        ),
        out_shape=[jax.ShapeDtypeStruct((m, n * tile), jnp.bfloat16)] * 2,
        **params(4 * m * k * n * tile, 4 * k * n * tile),
    )(order, a, gate, up)


def near_kernel(n, order, place, a, gate, up, gate_got, up_got, *outs):
    j = pl.program_id(0)
    gate_sum = product(a[...], gate[0]) + gate_got[...].astype(jnp.float32)
    up_sum = product(a[...], up[0]) + up_got[...].astype(jnp.float32)

    @pl.when(j < n)
    def _():
        outs[0][...] = gate_sum.astype(jnp.bfloat16)
        outs[1][...] = up_sum.astype(jnp.bfloat16)

    @pl.when(j >= n)
    def _():
        outs[2][...] = gate_sum
        outs[3][...] = up_sum


def project_near(a, gate, up, gate_got, up_got, order, place, tile):
    m, k = a.shape
    n = order.shape[0] // 2
    weight = pl.BlockSpec((1, k, tile), lambda j, order, place: (0, 0, order[j]))
    got = pl.BlockSpec((m, tile), lambda j, order, place: (0, place[j]))
    sent = pl.BlockSpec((m, tile), lambda j, order, place: (0, jnp.minimum(j, n - 1)))
    kept = pl.BlockSpec((m, tile), lambda j, order, place: (0, jnp.maximum(j - n, 0)))
    return pl.pallas_call(
        lambda *refs: near_kernel(n, *refs),
        grid_spec=pltpu.PrefetchScalarGridSpec(
            num_scalar_prefetch=2,
            grid=(2 * n,),
            in_specs=[
                pl.BlockSpec((m, k), lambda j, order, place: (0, 0)), weight, weight, got, got,
            ],
            out_specs=[sent, sent, kept, kept],
        ),
        out_shape=[jax.ShapeDtypeStruct((m, n * tile), jnp.bfloat16)] * 2
        + [jax.ShapeDtypeStruct((m, n * tile), jnp.float32)] * 2,
        **params(8 * m * k * n * tile, 8 * k * n * tile),
    )(order, place, a, gate, up, gate_got, up_got)


def down_kernel(a, weight, *refs):
    term = product(a[...], weight[0])
    if len(refs) == 2:
        term = term + refs[0][...]
    refs[-1][...] = term


def project_down(a, weight, chunk_index, total):
    m, k = a.shape
    width = weight.shape[2]
    tile = min(512, width)
    out = pl.BlockSpec((m, tile), lambda j: (0, j))
    adds = [] if total is None else [total]
    return pl.pallas_call(
        down_kernel,
        grid=(width // tile,),
        in_specs=[
            pl.BlockSpec((m, k), lambda j: (0, 0)),
            pl.BlockSpec((1, k, tile), lambda j: (0, chunk_index, j)),
        ]
        + [out] * len(adds),
        out_specs=out,
        out_shape=jax.ShapeDtypeStruct((m, width), jnp.float32),
        **params(2 * m * k * width, 2 * k * width),
    )(a, weight, *adds)


def shards(tokens, norm_gain, gate_weight, up_weight, down_weight):
    total = lax.axis_size("wide")
    position = lax.axis_index("wide")
    groups = total // WSPLIT
    rows, piece = tokens.shape
    width = norm_gain.shape[0]
    units = gate_weight.shape[2]
    lane, group = position % WSPLIT, position // WSPLIT
    core, side = position & 1, position >> 1 & 1
    gains = lax.dynamic_index_in_dim(
        norm_gain.reshape(groups, WSPLIT, piece), lane, 1, keepdims=False
    ).reshape(groups * piece)
    values = tokens.astype(jnp.float32)
    squares = jnp.sum(values * values, axis=1)
    for bit in range(total.bit_length() - 1):
        squares = squares + partner(squares, bit)
    inverse = lax.rsqrt(squares[:, None] / width + epsilon)

    chunk_rows = rows // ROW_CHUNKS
    unit_chunks = max(1, min(UNIT_CHUNKS, units // 512))
    chunk = units // unit_chunks
    half, quarter = chunk // 2, chunk // 4
    tile = min(256, quarter)
    per_half, per_quarter = half // tile, quarter // tile

    stages = [(r, c) for r in range(ROW_CHUNKS) for c in range(unit_chunks)]
    count = len(stages)
    previous = [tokens]
    normed, gots, state, hiddens = {}, {}, {}, {}
    results = [None] * ROW_CHUNKS
    outputs = [None] * ROW_CHUNKS

    def ordered(*values):
        tied, _ = lax.optimization_barrier((values, tuple(previous)))
        return tied

    def gather(r):
        (block,) = ordered(tokens[r * chunk_rows : (r + 1) * chunk_rows])
        mine = gather_groups(block, group, groups)
        scale = inverse[r * chunk_rows : (r + 1) * chunk_rows]
        normed[r] = (mine.astype(jnp.float32) * scale * gains).astype(jnp.bfloat16)

    def away(k):
        r, c = stages[k]
        (a,) = ordered(normed[r])
        first = (c * chunk + (1 - core) * half) // tile
        order = (first + jnp.arange(per_half)).astype(jnp.int32)
        gone = project_away(a, gate_weight, up_weight, order, tile)
        previous[:] = gone
        gots[k] = [partner(g, 0) for g in gone]

    def near(k):
        r, c = stages[k]
        (a,) = ordered(normed[r])
        steps = jnp.arange(per_quarter)
        place = jnp.concatenate(
            [(1 - side) * per_quarter + steps, side * per_quarter + steps]
        ).astype(jnp.int32)
        order = place + ((c * chunk + core * half) // tile).astype(jnp.int32)
        outs = project_near(a, gate_weight, up_weight, *gots.pop(k), order, place, tile)
        previous[:] = outs
        state[k] = outs[2:], [partner(o, 1) for o in outs[:2]]

    def activate(k):
        keep, back = state.pop(k)
        keep = ordered(*keep)
        sums = [x + y.astype(jnp.float32) for x, y in zip(keep, back)]
        hidden = (jax.nn.silu(sums[0]) * sums[1]).astype(jnp.bfloat16)
        previous[:] = [hidden]
        for bit in (1, 0):
            received = partner(hidden, bit)
            upper = position >> bit & 1 == 1
            hidden = jnp.concatenate(
                [jnp.where(upper, received, hidden), jnp.where(upper, hidden, received)],
                axis=1,
            )
        hiddens[k] = hidden

    def contract(k):
        r, c = stages[k]
        (hidden,) = ordered(hiddens.pop(k))
        results[r] = project_down(hidden, down_weight, c, results[r])
        previous[:] = [results[r]]
        if c == unit_chunks - 1:
            outputs[r] = scatter_groups(results[r], group, groups)

    gather(0)
    away(0)
    for k in range(count + 2):
        if k + 1 < count:
            away(k + 1)
        if k < count:
            near(k)
            r, c = stages[k]
            if c == 0 and r + 1 < ROW_CHUNKS:
                gather(r + 1)
        if 1 <= k <= count:
            activate(k - 1)
        if k >= 2:
            contract(k - 2)
    return jnp.concatenate(outputs, axis=0)


def solution(mesh):
    placed = (
        P("parts", "wide"),
        P(),
        P("wide", None, None),
        P("wide", None, None),
        P("wide", None, None),
    )
    return jax.shard_map(
        shards, mesh=mesh, in_specs=placed, out_specs=P("parts", "wide"), check_vma=False
    )
```

profile of v0, /device:TPU:0, one launch (start us, length us, event | category | flops | bytes accessed | tf_op | source)
XLA Modules:
  0.0 358.4 jit_solution(10059369421459406682)
XLA Ops:
  2.4 5.6 %collective-permute-start.3 = (bf16[256,512]{1,0:T(8,128)(2,1)S(1)}, bf16[256,512]{1,0:T(8,128)(2,1)S(1)}, u32[]{:S(2)}, u32[]{:S(2)}) collective-permute-start(bf16[256,512]{1,0:T(8,128)(2,1)S(1)} %get-tuple-element.95), channel_id=1, source_target_pairs={{0,4},{1,5},{2,6},{3,7},{4,8},{5,9},{6,10},{7,11},{8,12},{9,13},{1... | collective-permute-start | bytes 786440 | tf_op jit(solution)/shard_map/ppermute | solution.py:27
  13.6 4.6 %collective-permute-start.4 = (bf16[256,512]{1,0:T(8,128)(2,1)S(1)}, bf16[256,512]{1,0:T(8,128)(2,1)S(1)}, u32[]{:S(2)}, u32[]{:S(2)}) collective-permute-start(bf16[256,512]{1,0:T(8,128)(2,1)S(1)} %collective-permute-done.3), channel_id=1, source_target_pairs={{0,4},{1,5},{2,6},{3,7},{4,8},{5,9},{6,10},{7,11},{8,12},{9,13},{1... | collective-permute-start | bytes 786440 | tf_op jit(solution)/shard_map/ppermute | solution.py:27
  25.4 2.7 collective-permute-start.9
  29.5 4.6 %collective-permute-start.5 = (bf16[256,512]{1,0:T(8,128)(2,1)S(1)}, bf16[256,512]{1,0:T(8,128)(2,1)S(1)}, u32[]{:S(2)}, u32[]{:S(2)}) collective-permute-start(bf16[256,512]{1,0:T(8,128)(2,1)S(1)} %collective-permute-done.4), channel_id=1, source_target_pairs={{0,4},{1,5},{2,6},{3,7},{4,8},{5,9},{6,10},{7,11},{8,12},{9,13},{1... | collective-permute-start | bytes 786440 | tf_op jit(solution)/shard_map/ppermute | solution.py:27
  34.1 2.3 collective-permute-done.2
  38.9 6.2 %shard_map.55 = (bf16[256,1024]{1,0:T(8,128)(2,1)S(1)}, bf16[256,1024]{1,0:T(8,128)(2,1)S(1)}) custom-call(s32[4]{0:T(128)S(1)} %iota_add_fusion.3.order, bf16[256,2048]{1,0:T(8,128)(2,1)S(1)} %multiply_convert_fusion.1.a.refs_2_, bf16[1,2048,8192]{2,1,0:T(8,128)(2,1)} %refs_3_.15, bf16[1,2048,8192]{2,1,0:T(8,128)(2,1)} %refs_4_.15), custom_call_target="tpu_custom_call" | custom-call | flops 2147483648 | bytes 8388608 | tf_op jit(solution)/shard_map/pallas_call | solution.py:92
  45.6 6.2 %shard_map.56 = (bf16[256,1024]{1,0:T(8,128)(2,1)S(1)}, bf16[256,1024]{1,0:T(8,128)(2,1)S(1)}) custom-call(s32[4]{0:T(128)S(1)} %iota_add_fusion.2.order, bf16[256,2048]{1,0:T(8,128)(2,1)S(1)} %multiply_convert_fusion.1.a.refs_2_, bf16[1,2048,8192]{2,1,0:T(8,128)(2,1)} %refs_3_.15, bf16[1,2048,8192]{2,1,0:T(8,128)(2,1)} %refs_4_.15), custom_call_target="tpu_custom_call" | custom-call | flops 2147483648 | bytes 8388608 | tf_op jit(solution)/shard_map/pallas_call | solution.py:92
  52.4 6.4 %shard_map.57 = (bf16[256,512]{1,0:T(8,128)(2,1)S(1)}, bf16[256,512]{1,0:T(8,128)(2,1)S(1)}, f32[256,512]{1,0:T(8,128)S(1)}, f32[256,512]{1,0:T(8,128)S(1)}) custom-call(s32[4]{0:T(128)S(1)} %get-tuple-element.240.refs_0_, s32[4]{0:T(128)S(1)} %get-tuple-element.186.refs_1_, bf16[256,2048]{1,0:T(8,128)(2,1)S(1)} %multiply_convert_fusion.1.a.refs_2_, ...), custom_call_target="tpu_custom_call" | custom-call | flops 2147483648 | bytes 8388608 | tf_op jit(solution)/shard_map/pallas_call | solution.py:128
  60.9 6.2 %shard_map.58 = (bf16[256,1024]{1,0:T(8,128)(2,1)S(1)}, bf16[256,1024]{1,0:T(8,128)(2,1)S(1)}) custom-call(s32[4]{0:T(128)S(1)} %iota_add_fusion.1.order, bf16[256,2048]{1,0:T(8,128)(2,1)S(1)} %multiply_convert_fusion.1.a.refs_2_, bf16[1,2048,8192]{2,1,0:T(8,128)(2,1)} %refs_3_.15, bf16[1,2048,8192]{2,1,0:T(8,128)(2,1)} %refs_4_.15), custom_call_target="tpu_custom_call" | custom-call | flops 2147483648 | bytes 8388608 | tf_op jit(solution)/shard_map/pallas_call | solution.py:92
  69.1 6.4 %shard_map.59 = (bf16[256,512]{1,0:T(8,128)(2,1)S(1)}, bf16[256,512]{1,0:T(8,128)(2,1)S(1)}, f32[256,512]{1,0:T(8,128)S(1)}, f32[256,512]{1,0:T(8,128)S(1)}) custom-call(s32[4]{0:T(128)S(1)} %get-tuple-element.239.refs_0_, s32[4]{0:T(128)S(1)} %get-tuple-element.186.refs_1_, bf16[256,2048]{1,0:T(8,128)(2,1)S(1)} %multiply_convert_fusion.1.a.refs_2_, ...), custom_call_target="tpu_custom_call" | custom-call | flops 2147483648 | bytes 8388608 | tf_op jit(solution)/shard_map/pallas_call | solution.py:128
  75.6 5.0 %collective-permute-start.15 = (bf16[256,512]{1,0:T(8,128)(2,1)S(1)}, bf16[256,512]{1,0:T(8,128)(2,1)S(1)}, u32[]{:S(2)}, u32[]{:S(2)}) collective-permute-start(bf16[256,512]{1,0:T(8,128)(2,1)S(1)} %get-tuple-element.107), channel_id=1, source_target_pairs={{0,4},{1,5},{2,6},{3,7},{4,8},{5,9},{6,10},{7,11},{8,12},{9,13},{1... | collective-permute-start | bytes 786440 | tf_op jit(solution)/shard_map/ppermute | solution.py:27
  82.4 6.2 %shard_map.60 = (bf16[256,1024]{1,0:T(8,128)(2,1)S(1)}, bf16[256,1024]{1,0:T(8,128)(2,1)S(1)}) custom-call(s32[4]{0:T(128)S(1)} %iota_add_fusion.order, bf16[256,2048]{1,0:T(8,128)(2,1)S(1)} %multiply_convert_fusion.1.a.refs_2_, bf16[1,2048,8192]{2,1,0:T(8,128)(2,1)} %refs_3_.15, bf16[1,2048,8192]{2,1,0:T(8,128)(2,1)} %refs_4_.15), custom_call_target="tpu_custom_call" | custom-call | flops 2147483648 | bytes 8388608 | tf_op jit(solution)/shard_map/pallas_call | solution.py:92
  90.7 6.4 %shard_map.61 = (bf16[256,512]{1,0:T(8,128)(2,1)S(1)}, bf16[256,512]{1,0:T(8,128)(2,1)S(1)}, f32[256,512]{1,0:T(8,128)S(1)}, f32[256,512]{1,0:T(8,128)S(1)}) custom-call(s32[4]{0:T(128)S(1)} %get-tuple-element.185.refs_0_, s32[4]{0:T(128)S(1)} %get-tuple-element.186.refs_1_, bf16[256,2048]{1,0:T(8,128)(2,1)S(1)} %multiply_convert_fusion.1.a.refs_2_, ...), custom_call_target="tpu_custom_call" | custom-call | flops 2147483648 | bytes 8388608 | tf_op jit(solution)/shard_map/pallas_call | solution.py:128
  98.5 4.6 %collective-permute-start.16 = (bf16[256,512]{1,0:T(8,128)(2,1)S(1)}, bf16[256,512]{1,0:T(8,128)(2,1)S(1)}, u32[]{:S(2)}, u32[]{:S(2)}) collective-permute-start(bf16[256,512]{1,0:T(8,128)(2,1)S(1)} %collective-permute-done.15), channel_id=1, source_target_pairs={{0,4},{1,5},{2,6},{3,7},{4,8},{5,9},{6,10},{7,11},{8,12},{9,13},{1... | collective-permute-start | bytes 786440 | tf_op jit(solution)/shard_map/ppermute | solution.py:27
  104.0 4.1 %collective-permute-done.13 = bf16[256,512]{1,0:T(8,128)(2,1)S(1)} collective-permute-done((bf16[256,512]{1,0:T(8,128)(2,1)S(1)}, bf16[256,512]{1,0:T(8,128)(2,1)S(1)}, u32[]{:S(2)}, u32[]{:S(2)}) %collective-permute-start.13) | collective-permute-done | bytes 262176 | tf_op jit(solution)/shard_map/ppermute | solution.py:27
  109.4 4.6 %collective-permute-start.17 = (bf16[256,512]{1,0:T(8,128)(2,1)S(1)}, bf16[256,512]{1,0:T(8,128)(2,1)S(1)}, u32[]{:S(2)}, u32[]{:S(2)}) collective-permute-start(bf16[256,512]{1,0:T(8,128)(2,1)S(1)} %collective-permute-done.16), channel_id=1, source_target_pairs={{0,4},{1,5},{2,6},{3,7},{4,8},{5,9},{6,10},{7,11},{8,12},{9,13},{1... | collective-permute-start | bytes 786440 | tf_op jit(solution)/shard_map/ppermute | solution.py:27
  114.2 3.9 %collective-permute-done.14 = bf16[256,512]{1,0:T(8,128)(2,1)S(1)} collective-permute-done((bf16[256,512]{1,0:T(8,128)(2,1)S(1)}, bf16[256,512]{1,0:T(8,128)(2,1)S(1)}, u32[]{:S(2)}, u32[]{:S(2)}) %collective-permute-start.14) | collective-permute-done | bytes 262176 | tf_op jit(solution)/shard_map/ppermute | solution.py:27
  120.6 10.4 %collective-permute-done.30 = bf16[256,512]{1,0:T(8,128)(2,1)S(1)} collective-permute-done((bf16[256,512]{1,0:T(8,128)(2,1)S(1)}, bf16[256,512]{1,0:T(8,128)(2,1)S(1)}, u32[]{:S(2)}, u32[]{:S(2)}) %collective-permute-start.30) | collective-permute-done | bytes 262176 | tf_op jit(solution)/shard_map/ppermute | solution.py:17
  133.3 5.8 %shard_map.62.refs_0_ = f32[256,2048]{1,0:T(8,128)S(1)} custom-call(bf16[256,2048]{1,0:T(8,128)(2,1)S(1)} %pad_maximum_fusion.a, bf16[1,8192,2048]{2,1,0:T(8,128)(2,1)} %weight.15), custom_call_target="tpu_custom_call" | custom-call | flops 2147483648 | bytes 8388608 | tf_op jit(solution)/shard_map/pallas_call | solution.py:157
  139.1 6.2 %shard_map.63 = (bf16[256,1024]{1,0:T(8,128)(2,1)S(1)}, bf16[256,1024]{1,0:T(8,128)(2,1)S(1)}) custom-call(s32[4]{0:T(128)S(1)} %iota_add_fusion.3.order, bf16[256,2048]{1,0:T(8,128)(2,1)S(1)} %multiply_convert_fusion.a.refs_2_, bf16[1,2048,8192]{2,1,0:T(8,128)(2,1)} %refs_3_.15, bf16[1,2048,8192]{2,1,0:T(8,128)(2,1)} %refs_4_.15), custom_call_target="tpu_custom_call" | custom-call | flops 2147483648 | bytes 8388608 | tf_op jit(solution)/shard_map/pallas_call | solution.py:92
  145.9 6.4 %shard_map.64 = (bf16[256,512]{1,0:T(8,128)(2,1)S(1)}, bf16[256,512]{1,0:T(8,128)(2,1)S(1)}, f32[256,512]{1,0:T(8,128)S(1)}, f32[256,512]{1,0:T(8,128)S(1)}) custom-call(s32[4]{0:T(128)S(1)} %get-tuple-element.241.refs_0_, s32[4]{0:T(128)S(1)} %get-tuple-element.186.refs_1_, bf16[256,2048]{1,0:T(8,128)(2,1)S(1)} %multiply_convert_fusion.1.a.refs_2_, ...), custom_call_target="tpu_custom_call" | custom-call | flops 2147483648 | bytes 8388608 | tf_op jit(solution)/shard_map/pallas_call | solution.py:128
  155.5 5.7 %shard_map.65.refs_0_ = f32[256,2048]{1,0:T(8,128)S(1)} custom-call(bf16[256,2048]{1,0:T(8,128)(2,1)S(1)} %pad_maximum_fusion.1.a, bf16[1,8192,2048]{2,1,0:T(8,128)(2,1)} %weight.15, f32[256,2048]{1,0:T(8,128)S(1)} %shard_map.62.refs_0_), custom_call_target="tpu_custom_call" | custom-call | flops 2147483648 | bytes 8388608 | tf_op jit(solution)/shard_map/pallas_call | solution.py:157
  161.2 11.0 %collective-permute-done.40 = bf16[256,512]{1,0:T(8,128)(2,1)S(1)} collective-permute-done((bf16[256,512]{1,0:T(8,128)(2,1)S(1)}, bf16[256,512]{1,0:T(8,128)(2,1)S(1)}, u32[]{:S(2)}, u32[]{:S(2)}) %collective-permute-start.40) | collective-permute-done | bytes 262176 | tf_op jit(solution)/shard_map/ppermute | solution.py:17
  172.4 6.2 %shard_map.66 = (bf16[256,1024]{1,0:T(8,128)(2,1)S(1)}, bf16[256,1024]{1,0:T(8,128)(2,1)S(1)}) custom-call(s32[4]{0:T(128)S(1)} %iota_add_fusion.2.order, bf16[256,2048]{1,0:T(8,128)(2,1)S(1)} %multiply_convert_fusion.a.refs_2_, bf16[1,2048,8192]{2,1,0:T(8,128)(2,1)} %refs_3_.15, bf16[1,2048,8192]{2,1,0:T(8,128)(2,1)} %refs_4_.15), custom_call_target="tpu_custom_call" | custom-call | flops 2147483648 | bytes 8388608 | tf_op jit(solution)/shard_map/pallas_call | solution.py:92
  179.2 6.4 %shard_map.67 = (bf16[256,512]{1,0:T(8,128)(2,1)S(1)}, bf16[256,512]{1,0:T(8,128)(2,1)S(1)}, f32[256,512]{1,0:T(8,128)S(1)}, f32[256,512]{1,0:T(8,128)S(1)}) custom-call(s32[4]{0:T(128)S(1)} %get-tuple-element.240.refs_0_, s32[4]{0:T(128)S(1)} %get-tuple-element.186.refs_1_, bf16[256,2048]{1,0:T(8,128)(2,1)S(1)} %multiply_convert_fusion.a.refs_2_, ...), custom_call_target="tpu_custom_call" | custom-call | flops 2147483648 | bytes 8388608 | tf_op jit(solution)/shard_map/pallas_call | solution.py:128
  188.9 5.7 %shard_map.68.refs_0_ = f32[256,2048]{1,0:T(8,128)S(1)} custom-call(bf16[256,2048]{1,0:T(8,128)(2,1)S(1)} %pad_maximum_fusion.3.a, bf16[1,8192,2048]{2,1,0:T(8,128)(2,1)} %weight.15, f32[256,2048]{1,0:T(8,128)S(1)} %shard_map.65.refs_0_), custom_call_target="tpu_custom_call" | custom-call | flops 2147483648 | bytes 8388608 | tf_op jit(solution)/shard_map/pallas_call | solution.py:157
  194.6 6.2 %shard_map.69 = (bf16[256,1024]{1,0:T(8,128)(2,1)S(1)}, bf16[256,1024]{1,0:T(8,128)(2,1)S(1)}) custom-call(s32[4]{0:T(128)S(1)} %iota_add_fusion.1.order, bf16[256,2048]{1,0:T(8,128)(2,1)S(1)} %multiply_convert_fusion.a.refs_2_, bf16[1,2048,8192]{2,1,0:T(8,128)(2,1)} %refs_3_.15, bf16[1,2048,8192]{2,1,0:T(8,128)(2,1)} %refs_4_.15), custom_call_target="tpu_custom_call" | custom-call | flops 2147483648 | bytes 8388608 | tf_op jit(solution)/shard_map/pallas_call | solution.py:92
  200.7 6.4 %shard_map.70 = (bf16[256,512]{1,0:T(8,128)(2,1)S(1)}, bf16[256,512]{1,0:T(8,128)(2,1)S(1)}, f32[256,512]{1,0:T(8,128)S(1)}, f32[256,512]{1,0:T(8,128)S(1)}) custom-call(s32[4]{0:T(128)S(1)} %copy-done.9, s32[4]{0:T(128)S(1)} %get-tuple-element.186.refs_1_, bf16[256,2048]{1,0:T(8,128)(2,1)S(1)} %multiply_convert_fusion.a.refs_2_, ...), custom_call_target="tpu_custom_call" | custom-call | flops 2147483648 | bytes 8388608 | tf_op jit(solution)/shard_map/pallas_call | solution.py:128
  210.3 6.4 %collective-permute-done.52 = bf16[256,512]{1,0:T(8,128)(2,1)S(1)} collective-permute-done((bf16[256,512]{1,0:T(8,128)(2,1)S(1)}, bf16[256,512]{1,0:T(8,128)(2,1)S(1)}, u32[]{:S(2)}, u32[]{:S(2)}) %collective-permute-start.52) | collective-permute-done | bytes 262176 | tf_op jit(solution)/shard_map/ppermute | solution.py:17
  218.8 5.7 %shard_map.71 = f32[256,2048]{1,0:T(8,128)S(1)} custom-call(bf16[256,2048]{1,0:T(8,128)(2,1)S(1)} %pad_maximum_fusion.2.a, bf16[1,8192,2048]{2,1,0:T(8,128)(2,1)} %weight.15, f32[256,2048]{1,0:T(8,128)S(1)} %shard_map.68.refs_0_), custom_call_target="tpu_custom_call" | custom-call | flops 2147483648 | bytes 8388608 | tf_op jit(solution)/shard_map/pallas_call | solution.py:157
  224.5 6.2 %shard_map.72 = (bf16[256,1024]{1,0:T(8,128)(2,1)S(1)}, bf16[256,1024]{1,0:T(8,128)(2,1)S(1)}) custom-call(s32[4]{0:T(128)S(1)} %copy-done.11, bf16[256,2048]{1,0:T(8,128)(2,1)S(1)} %multiply_convert_fusion.a.refs_2_, bf16[1,2048,8192]{2,1,0:T(8,128)(2,1)} %refs_3_.15, bf16[1,2048,8192]{2,1,0:T(8,128)(2,1)} %refs_4_.15), custom_call_target="tpu_custom_call" | custom-call | flops 2147483648 | bytes 8388608 | tf_op jit(solution)/shard_map/pallas_call | solution.py:92
  231.3 6.4 %shard_map.73 = (bf16[256,512]{1,0:T(8,128)(2,1)S(1)}, bf16[256,512]{1,0:T(8,128)(2,1)S(1)}, f32[256,512]{1,0:T(8,128)S(1)}, f32[256,512]{1,0:T(8,128)S(1)}) custom-call(s32[4]{0:T(128)S(1)} %copy-done.5, s32[4]{0:T(128)S(1)} %get-tuple-element.186.refs_1_, bf16[256,2048]{1,0:T(8,128)(2,1)S(1)} %multiply_convert_fusion.a.refs_2_, ...), custom_call_target="tpu_custom_call" | custom-call | flops 2147483648 | bytes 8388608 | tf_op jit(solution)/shard_map/pallas_call | solution.py:128
  240.9 16.7 %collective-permute-done.60 = bf16[256,512]{1,0:T(8,128)(2,1)S(1)} collective-permute-done((bf16[256,512]{1,0:T(8,128)(2,1)S(1)}, bf16[256,512]{1,0:T(8,128)(2,1)S(1)}, u32[]{:S(2)}, u32[]{:S(2)}) %collective-permute-start.60) | collective-permute-done | bytes 262176 | tf_op jit(solution)/shard_map/ppermute | solution.py:17
  257.9 5.6 %shard_map.74.refs_0_ = f32[256,2048]{1,0:T(8,128)S(1)} custom-call(bf16[256,2048]{1,0:T(8,128)(2,1)S(1)} %pad_maximum_fusion.4.a, bf16[1,8192,2048]{2,1,0:T(8,128)(2,1)} %weight.15), custom_call_target="tpu_custom_call" | custom-call | flops 2147483648 | bytes 8388608 | tf_op jit(solution)/shard_map/pallas_call | solution.py:157
  263.6 6.6 %shard_map.75 = (bf16[256,512]{1,0:T(8,128)(2,1)S(1)}, bf16[256,512]{1,0:T(8,128)(2,1)S(1)}, f32[256,512]{1,0:T(8,128)S(1)}, f32[256,512]{1,0:T(8,128)S(1)}) custom-call(s32[4]{0:T(128)S(1)} %copy-done.7, s32[4]{0:T(128)S(1)} %get-tuple-element.186.refs_1_, bf16[256,2048]{1,0:T(8,128)(2,1)S(1)} %multiply_convert_fusion.a.refs_2_, ...), custom_call_target="tpu_custom_call" | custom-call | flops 2147483648 | bytes 8388608 | tf_op jit(solution)/shard_map/pallas_call | solution.py:128
  273.4 5.7 %shard_map.76.refs_0_ = f32[256,2048]{1,0:T(8,128)S(1)} custom-call(bf16[256,2048]{1,0:T(8,128)(2,1)S(1)} %pad_maximum_fusion.5.a, bf16[1,8192,2048]{2,1,0:T(8,128)(2,1)} %weight.15, f32[256,2048]{1,0:T(8,128)S(1)} %shard_map.74.refs_0_), custom_call_target="tpu_custom_call" | custom-call | flops 2147483648 | bytes 8388608 | tf_op jit(solution)/shard_map/pallas_call | solution.py:157
  280.4 4.6 %collective-permute-done.65 = bf16[256,512]{1,0:T(8,128)(2,1)S(1)} collective-permute-done((bf16[256,512]{1,0:T(8,128)(2,1)S(1)}, bf16[256,512]{1,0:T(8,128)(2,1)S(1)}, u32[]{:S(2)}, u32[]{:S(2)}) %collective-permute-start.65) | collective-permute-done | bytes 262176 | tf_op jit(solution)/shard_map/ppermute | solution.py:17
  285.8 4.8 %collective-permute-done.68 = bf16[256,512]{1,0:T(8,128)(2,1)S(1)} collective-permute-done((bf16[256,512]{1,0:T(8,128)(2,1)S(1)}, bf16[256,512]{1,0:T(8,128)(2,1)S(1)}, u32[]{:S(2)}, u32[]{:S(2)}) %collective-permute-start.68) | collective-permute-done | bytes 262176 | tf_op jit(solution)/shard_map/ppermute | solution.py:17
  292.4 3.9 %collective-permute-start.46 = (bf16[256,512]{1,0:T(8,128)(2,1)}, bf16[256,512]{1,0:T(8,128)(2,1)}, u32[]{:S(2)}, u32[]{:S(2)}) collective-permute-start(bf16[256,512]{1,0:T(8,128)(2,1)} %get-tuple-element.189), channel_id=1, source_target_pairs={{0,4},{1,5},{2,6},{3,7},{16,20},{17,21},{18,22},{19,23}} | collective-permute-start | bytes 786440 | tf_op jit(solution)/shard_map/ppermute | solution.py:27
  299.0 5.7 %shard_map.77.refs_0_ = f32[256,2048]{1,0:T(8,128)S(1)} custom-call(bf16[256,2048]{1,0:T(8,128)(2,1)S(1)} %pad_maximum_fusion.7.a, bf16[1,8192,2048]{2,1,0:T(8,128)(2,1)} %weight.15, f32[256,2048]{1,0:T(8,128)S(1)} %copy-done.3), custom_call_target="tpu_custom_call" | custom-call | flops 2147483648 | bytes 8388608 | tf_op jit(solution)/shard_map/pallas_call | solution.py:157
  305.0 5.7 %shard_map.78 = f32[256,2048]{1,0:T(8,128)S(1)} custom-call(bf16[256,2048]{1,0:T(8,128)(2,1)S(1)} %pad_maximum_fusion.6.a, bf16[1,8192,2048]{2,1,0:T(8,128)(2,1)} %weight.15, f32[256,2048]{1,0:T(8,128)S(1)} %shard_map.77.refs_0_), custom_call_target="tpu_custom_call" | custom-call | flops 2147483648 | bytes 8388608 | tf_op jit(solution)/shard_map/pallas_call | solution.py:157
  312.1 2.8 collective-permute-start.70
  317.4 2.0 collective-permute-start.47
  322.8 4.4 %collective-permute-start.71 = (bf16[256,512]{1,0:T(8,128)(2,1)S(1)}, bf16[256,512]{1,0:T(8,128)(2,1)S(1)}, u32[]{:S(2)}, u32[]{:S(2)}) collective-permute-start(bf16[256,512]{1,0:T(8,128)(2,1)S(1)} %add_convert_fusion.4), channel_id=1, source_target_pairs={{0,4},{1,5},{2,6},{3,7},{4,8},{5,9},{6,10},{7,11},{16,20},{17,21},... | collective-permute-start | bytes 786440 | tf_op jit(solution)/shard_map/ppermute | solution.py:27
  327.2 2.1 add_convert_fusion.8
  334.9 4.3 %collective-permute-start.48 = (bf16[256,512]{1,0:T(8,128)(2,1)}, bf16[256,512]{1,0:T(8,128)(2,1)S(1)}, u32[]{:S(2)}, u32[]{:S(2)}) collective-permute-start(bf16[256,512]{1,0:T(8,128)(2,1)} %get-tuple-element.187), channel_id=1, source_target_pairs={{0,4},{1,5},{2,6},{3,7},{4,8},{5,9},{6,10},{7,11},{8,12},{9,13},{1... | collective-permute-start | bytes 786440 | tf_op jit(solution)/shard_map/ppermute | solution.py:27
  340.6 5.2 %collective-permute-start.72 = (bf16[256,512]{1,0:T(8,128)(2,1)}, bf16[256,512]{1,0:T(8,128)(2,1)S(1)}, u32[]{:S(2)}, u32[]{:S(2)}) collective-permute-start(bf16[256,512]{1,0:T(8,128)(2,1)} %get-tuple-element.191), channel_id=1, source_target_pairs={{0,4},{1,5},{2,6},{3,7},{4,8},{5,9},{6,10},{7,11},{8,12},{9,13},{1... | collective-permute-start | bytes 786440 | tf_op jit(solution)/shard_map/ppermute | solution.py:27
  350.0 6.4 %collective-permute-done.75 = bf16[256,512]{1,0:T(8,128)(2,1)S(1)} collective-permute-done((bf16[256,512]{1,0:T(8,128)(2,1)}, bf16[256,512]{1,0:T(8,128)(2,1)S(1)}, u32[]{:S(2)}, u32[]{:S(2)}) %collective-permute-start.75) | collective-permute-done | bytes 262176 | tf_op jit(solution)/shard_map/ppermute | solution.py:27
  (234 shorter events, 83.6 us)
Async XLA Ops:
  1.1 11.2 %collective-permute-start = (bf16[256,512]{1,0:T(8,128)(2,1)S(1)}, bf16[256,512]{1,0:T(8,128)(2,1)S(1)}, u32[]{:S(2)}, u32[]{:S(2)}) collective-permute-start(bf16[256,512]{1,0:T(8,128)(2,1)S(1)} %get-tuple-element.95), channel_id=1, source_target_pairs={{4,0},{5,1},{6,2},{7,3},{8,4},{9,5},{10,6},{11,7},{12,8},{13,9},{1... | collective-permute-start | bytes 786440 | tf_op jit(solution)/shard_map/ppermute | solution.py:27
  12.3 15.9 %collective-permute-start.1 = (bf16[256,512]{1,0:T(8,128)(2,1)S(1)}, bf16[256,512]{1,0:T(8,128)(2,1)S(1)}, u32[]{:S(2)}, u32[]{:S(2)}) collective-permute-start(bf16[256,512]{1,0:T(8,128)(2,1)S(1)} %collective-permute-done), channel_id=1, source_target_pairs={{4,0},{5,1},{6,2},{7,3},{8,4},{9,5},{10,6},{11,7},{12,8},{13,9},{1... | collective-permute-start | bytes 786440 | tf_op jit(solution)/shard_map/ppermute | solution.py:27
  13.6 15.9 %collective-permute-start.4 = (bf16[256,512]{1,0:T(8,128)(2,1)S(1)}, bf16[256,512]{1,0:T(8,128)(2,1)S(1)}, u32[]{:S(2)}, u32[]{:S(2)}) collective-permute-start(bf16[256,512]{1,0:T(8,128)(2,1)S(1)} %collective-permute-done.3), channel_id=1, source_target_pairs={{0,4},{1,5},{2,6},{3,7},{4,8},{5,9},{6,10},{7,11},{8,12},{9,13},{1... | collective-permute-start | bytes 786440 | tf_op jit(solution)/shard_map/ppermute | solution.py:27
  51.8 15.5 %collective-permute-start.18 = (bf16[256,1024]{1,0:T(8,128)(2,1)S(1)}, bf16[256,1024]{1,0:T(8,128)(2,1)S(1)}, u32[]{:S(2)}, u32[]{:S(2)}) collective-permute-start(bf16[256,1024]{1,0:T(8,128)(2,1)S(1)} %get-tuple-element.100), channel_id=1, source_target_pairs={{0,1},{1,0},{2,3},{3,2},{4,5},{5,4},{6,7},{7,6},{8,9},{9,8},{10,11... | collective-permute-start | bytes 1572872 | tf_op jit(solution)/shard_map/ppermute | solution.py:17
  51.9 15.9 %collective-permute-start.19 = (bf16[256,1024]{1,0:T(8,128)(2,1)S(1)}, bf16[256,1024]{1,0:T(8,128)(2,1)S(1)}, u32[]{:S(2)}, u32[]{:S(2)}) collective-permute-start(bf16[256,1024]{1,0:T(8,128)(2,1)S(1)} %get-tuple-element.101), channel_id=1, source_target_pairs={{0,1},{1,0},{2,3},{3,2},{4,5},{5,4},{6,7},{7,6},{8,9},{9,8},{10,11... | collective-permute-start | bytes 1572872 | tf_op jit(solution)/shard_map/ppermute | solution.py:17
  58.8 16.8 %collective-permute-start.20 = (bf16[256,512]{1,0:T(8,128)(2,1)S(1)}, bf16[256,512]{1,0:T(8,128)(2,1)S(1)}, u32[]{:S(2)}, u32[]{:S(2)}) collective-permute-start(bf16[256,512]{1,0:T(8,128)(2,1)S(1)} %get-tuple-element.103), channel_id=1, source_target_pairs={{0,2},{1,3},{2,0},{3,1},{4,6},{5,7},{6,4},{7,5},{8,10},{9,11},{10,... | collective-permute-start | bytes 786440 | tf_op jit(solution)/shard_map/ppermute | solution.py:17
  60.4 20.2 %collective-permute-start.21 = (bf16[256,512]{1,0:T(8,128)(2,1)S(1)}, bf16[256,512]{1,0:T(8,128)(2,1)S(1)}, u32[]{:S(2)}, u32[]{:S(2)}) collective-permute-start(bf16[256,512]{1,0:T(8,128)(2,1)S(1)} %get-tuple-element.104), channel_id=1, source_target_pairs={{0,2},{1,3},{2,0},{3,1},{4,6},{5,7},{6,4},{7,5},{8,10},{9,11},{10,... | collective-permute-start | bytes 786440 | tf_op jit(solution)/shard_map/ppermute | solution.py:17
  67.1 21.5 %collective-permute-start.24 = (bf16[256,1024]{1,0:T(8,128)(2,1)S(1)}, bf16[256,1024]{1,0:T(8,128)(2,1)S(1)}, u32[]{:S(2)}, u32[]{:S(2)}) collective-permute-start(bf16[256,1024]{1,0:T(8,128)(2,1)S(1)} %get-tuple-element.109), channel_id=1, source_target_pairs={{0,1},{1,0},{2,3},{3,2},{4,5},{5,4},{6,7},{7,6},{8,9},{9,8},{10,11... | collective-permute-start | bytes 1572872 | tf_op jit(solution)/shard_map/ppermute | solution.py:17
  67.3 21.9 %collective-permute-start.25 = (bf16[256,1024]{1,0:T(8,128)(2,1)S(1)}, bf16[256,1024]{1,0:T(8,128)(2,1)S(1)}, u32[]{:S(2)}, u32[]{:S(2)}) collective-permute-start(bf16[256,1024]{1,0:T(8,128)(2,1)S(1)} %get-tuple-element.110), channel_id=1, source_target_pairs={{0,1},{1,0},{2,3},{3,2},{4,5},{5,4},{6,7},{7,6},{8,9},{9,8},{10,11... | collective-permute-start | bytes 1572872 | tf_op jit(solution)/shard_map/ppermute | solution.py:17
  67.8 29.3 %collective-permute-start.12 = (bf16[256,512]{1,0:T(8,128)(2,1)S(1)}, bf16[256,512]{1,0:T(8,128)(2,1)S(1)}, u32[]{:S(2)}, u32[]{:S(2)}) collective-permute-start(bf16[256,512]{1,0:T(8,128)(2,1)S(1)} %get-tuple-element.107), channel_id=1, source_target_pairs={{4,0},{5,1},{6,2},{7,3},{8,4},{9,5},{10,6},{11,7},{12,8},{13,9},{1... | collective-permute-start | bytes 786440 | tf_op jit(solution)/shard_map/ppermute | solution.py:27
  75.6 21.6 %collective-permute-start.15 = (bf16[256,512]{1,0:T(8,128)(2,1)S(1)}, bf16[256,512]{1,0:T(8,128)(2,1)S(1)}, u32[]{:S(2)}, u32[]{:S(2)}) collective-permute-start(bf16[256,512]{1,0:T(8,128)(2,1)S(1)} %get-tuple-element.107), channel_id=1, source_target_pairs={{0,4},{1,5},{2,6},{3,7},{4,8},{5,9},{6,10},{7,11},{8,12},{9,13},{1... | collective-permute-start | bytes 786440 | tf_op jit(solution)/shard_map/ppermute | solution.py:27
  80.8 17.7 %collective-permute-start.22 = (bf16[256,512]{1,0:T(8,128)(2,1)S(1)}, bf16[256,512]{1,0:T(8,128)(2,1)S(1)}, u32[]{:S(2)}, u32[]{:S(2)}) collective-permute-start(bf16[256,512]{1,0:T(8,128)(2,1)S(1)} %multiply_convert_fusion.9), channel_id=1, source_target_pairs={{0,2},{1,3},{2,0},{3,1},{4,6},{5,7},{6,4},{7,5},{8,10},{9,11},{10,... | collective-permute-start | bytes 786440 | tf_op jit(solution)/shard_map/ppermute | solution.py:17
  88.6 14.6 %collective-permute-start.26 = (bf16[256,512]{1,0:T(8,128)(2,1)S(1)}, bf16[256,512]{1,0:T(8,128)(2,1)S(1)}, u32[]{:S(2)}, u32[]{:S(2)}) collective-permute-start(bf16[256,512]{1,0:T(8,128)(2,1)S(1)} %get-tuple-element.112), channel_id=1, source_target_pairs={{0,2},{1,3},{2,0},{3,1},{4,6},{5,7},{6,4},{7,5},{8,10},{9,11},{10,... | collective-permute-start | bytes 786440 | tf_op jit(solution)/shard_map/ppermute | solution.py:17
  89.2 14.3 %collective-permute-start.27 = (bf16[256,512]{1,0:T(8,128)(2,1)S(1)}, bf16[256,512]{1,0:T(8,128)(2,1)S(1)}, u32[]{:S(2)}, u32[]{:S(2)}) collective-permute-start(bf16[256,512]{1,0:T(8,128)(2,1)S(1)} %get-tuple-element.113), channel_id=1, source_target_pairs={{0,2},{1,3},{2,0},{3,1},{4,6},{5,7},{6,4},{7,5},{8,10},{9,11},{10,... | collective-permute-start | bytes 786440 | tf_op jit(solution)/shard_map/ppermute | solution.py:17
  97.1 48.2 %collective-permute-start.28 = (bf16[256,1024]{1,0:T(8,128)(2,1)S(1)}, bf16[256,1024]{1,0:T(8,128)(2,1)S(1)}, u32[]{:S(2)}, u32[]{:S(2)}) collective-permute-start(bf16[256,1024]{1,0:T(8,128)(2,1)S(1)} %get-tuple-element.119), channel_id=1, source_target_pairs={{0,1},{1,0},{2,3},{3,2},{4,5},{5,4},{6,7},{7,6},{8,9},{9,8},{10,11... | collective-permute-start | bytes 1572872 | tf_op jit(solution)/shard_map/ppermute | solution.py:17
  103.2 42.5 %collective-permute-start.29 = (bf16[256,1024]{1,0:T(8,128)(2,1)S(1)}, bf16[256,1024]{1,0:T(8,128)(2,1)S(1)}, u32[]{:S(2)}, u32[]{:S(2)}) collective-permute-start(bf16[256,1024]{1,0:T(8,128)(2,1)S(1)} %get-tuple-element.120), channel_id=1, source_target_pairs={{0,1},{1,0},{2,3},{3,2},{4,5},{5,4},{6,7},{7,6},{8,9},{9,8},{10,11... | collective-permute-start | bytes 1572872 | tf_op jit(solution)/shard_map/ppermute | solution.py:17
  103.5 48.8 %collective-permute-start.32 = (bf16[256,512]{1,0:T(8,128)(2,1)S(1)}, bf16[256,512]{1,0:T(8,128)(2,1)S(1)}, u32[]{:S(2)}, u32[]{:S(2)}) collective-permute-start(bf16[256,512]{1,0:T(8,128)(2,1)S(1)} %get-tuple-element.122), channel_id=1, source_target_pairs={{0,2},{1,3},{2,0},{3,1},{4,6},{5,7},{6,4},{7,5},{8,10},{9,11},{10,... | collective-permute-start | bytes 786440 | tf_op jit(solution)/shard_map/ppermute | solution.py:17
  118.1 34.8 %collective-permute-start.33 = (bf16[256,512]{1,0:T(8,128)(2,1)S(1)}, bf16[256,512]{1,0:T(8,128)(2,1)S(1)}, u32[]{:S(2)}, u32[]{:S(2)}) collective-permute-start(bf16[256,512]{1,0:T(8,128)(2,1)S(1)} %get-tuple-element.123), channel_id=1, source_target_pairs={{0,2},{1,3},{2,0},{3,1},{4,6},{5,7},{6,4},{7,5},{8,10},{9,11},{10,... | collective-permute-start | bytes 786440 | tf_op jit(solution)/shard_map/ppermute | solution.py:17
  119.3 11.7 %collective-permute-start.30 = (bf16[256,512]{1,0:T(8,128)(2,1)S(1)}, bf16[256,512]{1,0:T(8,128)(2,1)S(1)}, u32[]{:S(2)}, u32[]{:S(2)}) collective-permute-start(bf16[256,512]{1,0:T(8,128)(2,1)S(1)} %multiply_convert_fusion.8), channel_id=1, source_target_pairs={{0,2},{1,3},{2,0},{3,1},{4,6},{5,7},{6,4},{7,5},{8,10},{9,11},{10,... | collective-permute-start | bytes 786440 | tf_op jit(solution)/shard_map/ppermute | solution.py:17
  132.8 21.8 %collective-permute-start.31 = (bf16[256,1024]{1,0:T(8,128)(2,1)S(1)}, bf16[256,1024]{1,0:T(8,128)(2,1)S(1)}, u32[]{:S(2)}, u32[]{:S(2)}) collective-permute-start(bf16[256,1024]{1,0:T(8,128)(2,1)S(1)} %pad_maximum_fusion.9), channel_id=1, source_target_pairs={{0,1},{1,0},{2,3},{3,2},{4,5},{5,4},{6,7},{7,6},{8,9},{9,8},{10,11... | collective-permute-start | bytes 1572872 | tf_op jit(solution)/shard_map/ppermute | solution.py:17
  145.3 33.3 %collective-permute-start.34 = (bf16[256,1024]{1,0:T(8,128)(2,1)S(1)}, bf16[256,1024]{1,0:T(8,128)(2,1)S(1)}, u32[]{:S(2)}, u32[]{:S(2)}) collective-permute-start(bf16[256,1024]{1,0:T(8,128)(2,1)S(1)} %get-tuple-element.130), channel_id=1, source_target_pairs={{0,1},{1,0},{2,3},{3,2},{4,5},{5,4},{6,7},{7,6},{8,9},{9,8},{10,11... | collective-permute-start | bytes 1572872 | tf_op jit(solution)/shard_map/ppermute | solution.py:17
  145.7 33.4 %collective-permute-start.35 = (bf16[256,1024]{1,0:T(8,128)(2,1)S(1)}, bf16[256,1024]{1,0:T(8,128)(2,1)S(1)}, u32[]{:S(2)}, u32[]{:S(2)}) collective-permute-start(bf16[256,1024]{1,0:T(8,128)(2,1)S(1)} %get-tuple-element.131), channel_id=1, source_target_pairs={{0,1},{1,0},{2,3},{3,2},{4,5},{5,4},{6,7},{7,6},{8,9},{9,8},{10,11... | collective-permute-start | bytes 1572872 | tf_op jit(solution)/shard_map/ppermute | solution.py:17
  152.3 33.3 %collective-permute-start.36 = (bf16[256,512]{1,0:T(8,128)(2,1)S(1)}, bf16[256,512]{1,0:T(8,128)(2,1)S(1)}, u32[]{:S(2)}, u32[]{:S(2)}) collective-permute-start(bf16[256,512]{1,0:T(8,128)(2,1)S(1)} %get-tuple-element.135), channel_id=1, source_target_pairs={{0,2},{1,3},{2,0},{3,1},{4,6},{5,7},{6,4},{7,5},{8,10},{9,11},{10,... | collective-permute-start | bytes 786440 | tf_op jit(solution)/shard_map/ppermute | solution.py:17
  152.9 33.3 %collective-permute-start.37 = (bf16[256,512]{1,0:T(8,128)(2,1)S(1)}, bf16[256,512]{1,0:T(8,128)(2,1)S(1)}, u32[]{:S(2)}, u32[]{:S(2)}) collective-permute-start(bf16[256,512]{1,0:T(8,128)(2,1)S(1)} %get-tuple-element.136), channel_id=1, source_target_pairs={{0,2},{1,3},{2,0},{3,1},{4,6},{5,7},{6,4},{7,5},{8,10},{9,11},{10,... | collective-permute-start | bytes 786440 | tf_op jit(solution)/shard_map/ppermute | solution.py:17
  154.6 17.6 %collective-permute-start.40 = (bf16[256,512]{1,0:T(8,128)(2,1)S(1)}, bf16[256,512]{1,0:T(8,128)(2,1)S(1)}, u32[]{:S(2)}, u32[]{:S(2)}) collective-permute-start(bf16[256,512]{1,0:T(8,128)(2,1)S(1)} %multiply_convert_fusion.7), channel_id=1, source_target_pairs={{0,2},{1,3},{2,0},{3,1},{4,6},{5,7},{6,4},{7,5},{8,10},{9,11},{10,... | collective-permute-start | bytes 786440 | tf_op jit(solution)/shard_map/ppermute | solution.py:17
  172.3 15.6 %collective-permute-start.41 = (bf16[256,1024]{1,0:T(8,128)(2,1)S(1)}, bf16[256,1024]{1,0:T(8,128)(2,1)S(1)}, u32[]{:S(2)}, u32[]{:S(2)}) collective-permute-start(bf16[256,1024]{1,0:T(8,128)(2,1)S(1)} %pad_maximum_fusion.11), channel_id=1, source_target_pairs={{0,1},{1,0},{2,3},{3,2},{4,5},{5,4},{6,7},{7,6},{8,9},{9,8},{10,11... | collective-permute-start | bytes 1572872 | tf_op jit(solution)/shard_map/ppermute | solution.py:17
  178.6 22.2 %collective-permute-start.42 = (bf16[256,1024]{1,0:T(8,128)(2,1)S(1)}, bf16[256,1024]{1,0:T(8,128)(2,1)S(1)}, u32[]{:S(2)}, u32[]{:S(2)}) collective-permute-start(bf16[256,1024]{1,0:T(8,128)(2,1)S(1)} %get-tuple-element.141), channel_id=1, source_target_pairs={{0,1},{1,0},{2,3},{3,2},{4,5},{5,4},{6,7},{7,6},{8,9},{9,8},{10,11... | collective-permute-start | bytes 1572872 | tf_op jit(solution)/shard_map/ppermute | solution.py:17
  179.1 21.6 %collective-permute-start.43 = (bf16[256,1024]{1,0:T(8,128)(2,1)S(1)}, bf16[256,1024]{1,0:T(8,128)(2,1)S(1)}, u32[]{:S(2)}, u32[]{:S(2)}) collective-permute-start(bf16[256,1024]{1,0:T(8,128)(2,1)S(1)} %get-tuple-element.142), channel_id=1, source_target_pairs={{0,1},{1,0},{2,3},{3,2},{4,5},{5,4},{6,7},{7,6},{8,9},{9,8},{10,11... | collective-permute-start | bytes 1572872 | tf_op jit(solution)/shard_map/ppermute | solution.py:17
  185.6 21.5 %collective-permute-start.44 = (bf16[256,512]{1,0:T(8,128)(2,1)S(1)}, bf16[256,512]{1,0:T(8,128)(2,1)S(1)}, u32[]{:S(2)}, u32[]{:S(2)}) collective-permute-start(bf16[256,512]{1,0:T(8,128)(2,1)S(1)} %get-tuple-element.144), channel_id=1, source_target_pairs={{0,2},{1,3},{2,0},{3,1},{4,6},{5,7},{6,4},{7,5},{8,10},{9,11},{10,... | collective-permute-start | bytes 786440 | tf_op jit(solution)/shard_map/ppermute | solution.py:17
  186.2 21.0 %collective-permute-start.45 = (bf16[256,512]{1,0:T(8,128)(2,1)S(1)}, bf16[256,512]{1,0:T(8,128)(2,1)S(1)}, u32[]{:S(2)}, u32[]{:S(2)}) collective-permute-start(bf16[256,512]{1,0:T(8,128)(2,1)S(1)} %get-tuple-element.145), channel_id=1, source_target_pairs={{0,2},{1,3},{2,0},{3,1},{4,6},{5,7},{6,4},{7,5},{8,10},{9,11},{10,... | collective-permute-start | bytes 786440 | tf_op jit(solution)/shard_map/ppermute | solution.py:17
  188.0 21.0 %collective-permute-start.38 = (bf16[256,512]{1,0:T(8,128)(2,1)S(1)}, bf16[256,512]{1,0:T(8,128)(2,1)S(1)}, u32[]{:S(2)}, u32[]{:S(2)}) collective-permute-start(bf16[256,512]{1,0:T(8,128)(2,1)S(1)} %multiply_convert_fusion.6), channel_id=1, source_target_pairs={{0,2},{1,3},{2,0},{3,1},{4,6},{5,7},{6,4},{7,5},{8,10},{9,11},{10,... | collective-permute-start | bytes 786440 | tf_op jit(solution)/shard_map/ppermute | solution.py:17
  209.2 21.4 %collective-permute-start.54 = (bf16[256,1024]{1,0:T(8,128)(2,1)S(1)}, bf16[256,1024]{1,0:T(8,128)(2,1)S(1)}, u32[]{:S(2)}, u32[]{:S(2)}) collective-permute-start(bf16[256,1024]{1,0:T(8,128)(2,1)S(1)} %get-tuple-element.152), channel_id=1, source_target_pairs={{0,1},{1,0},{2,3},{3,2},{4,5},{5,4},{6,7},{7,6},{8,9},{9,8},{10,11... | collective-permute-start | bytes 1572872 | tf_op jit(solution)/shard_map/ppermute | solution.py:17
  209.7 21.5 %collective-permute-start.55 = (bf16[256,1024]{1,0:T(8,128)(2,1)S(1)}, bf16[256,1024]{1,0:T(8,128)(2,1)S(1)}, u32[]{:S(2)}, u32[]{:S(2)}) collective-permute-start(bf16[256,1024]{1,0:T(8,128)(2,1)S(1)} %get-tuple-element.153), channel_id=1, source_target_pairs={{0,1},{1,0},{2,3},{3,2},{4,5},{5,4},{6,7},{7,6},{8,9},{9,8},{10,11... | collective-permute-start | bytes 1572872 | tf_op jit(solution)/shard_map/ppermute | solution.py:17
  209.8 28.0 %collective-permute-start.56 = (bf16[256,512]{1,0:T(8,128)(2,1)S(1)}, bf16[256,512]{1,0:T(8,128)(2,1)S(1)}, u32[]{:S(2)}, u32[]{:S(2)}) collective-permute-start(bf16[256,512]{1,0:T(8,128)(2,1)S(1)} %get-tuple-element.155), channel_id=1, source_target_pairs={{0,2},{1,3},{2,0},{3,1},{4,6},{5,7},{6,4},{7,5},{8,10},{9,11},{10,... | collective-permute-start | bytes 786440 | tf_op jit(solution)/shard_map/ppermute | solution.py:17
  216.7 21.6 %collective-permute-start.57 = (bf16[256,512]{1,0:T(8,128)(2,1)S(1)}, bf16[256,512]{1,0:T(8,128)(2,1)S(1)}, u32[]{:S(2)}, u32[]{:S(2)}) collective-permute-start(bf16[256,512]{1,0:T(8,128)(2,1)S(1)} %get-tuple-element.156), channel_id=1, source_target_pairs={{0,2},{1,3},{2,0},{3,1},{4,6},{5,7},{6,4},{7,5},{8,10},{9,11},{10,... | collective-permute-start | bytes 786440 | tf_op jit(solution)/shard_map/ppermute | solution.py:17
  218.3 21.7 %collective-permute-start.53 = (bf16[256,1024]{1,0:T(8,128)(2,1)S(1)}, bf16[256,1024]{1,0:T(8,128)(2,1)S(1)}, u32[]{:S(2)}, u32[]{:S(2)}) collective-permute-start(bf16[256,1024]{1,0:T(8,128)(2,1)S(1)} %pad_maximum_fusion.12), channel_id=1, source_target_pairs={{0,1},{1,0},{2,3},{3,2},{4,5},{5,4},{6,7},{7,6},{8,9},{9,8},{10,11... | collective-permute-start | bytes 1572872 | tf_op jit(solution)/shard_map/ppermute | solution.py:17
  230.6 32.9 %collective-permute-start.58 = (bf16[256,1024]{1,0:T(8,128)(2,1)S(1)}, bf16[256,1024]{1,0:T(8,128)(2,1)S(1)}, u32[]{:S(2)}, u32[]{:S(2)}) collective-permute-start(bf16[256,1024]{1,0:T(8,128)(2,1)S(1)} %get-tuple-element.163), channel_id=1, source_target_pairs={{0,1},{1,0},{2,3},{3,2},{4,5},{5,4},{6,7},{7,6},{8,9},{9,8},{10,11... | collective-permute-start | bytes 1572872 | tf_op jit(solution)/shard_map/ppermute | solution.py:17
  231.2 32.3 %collective-permute-start.59 = (bf16[256,1024]{1,0:T(8,128)(2,1)S(1)}, bf16[256,1024]{1,0:T(8,128)(2,1)S(1)}, u32[]{:S(2)}, u32[]{:S(2)}) collective-permute-start(bf16[256,1024]{1,0:T(8,128)(2,1)S(1)} %get-tuple-element.164), channel_id=1, source_target_pairs={{0,1},{1,0},{2,3},{3,2},{4,5},{5,4},{6,7},{7,6},{8,9},{9,8},{10,11... | collective-permute-start | bytes 1572872 | tf_op jit(solution)/shard_map/ppermute | solution.py:17
  237.7 34.6 %collective-permute-start.62 = (bf16[256,512]{1,0:T(8,128)(2,1)S(1)}, bf16[256,512]{1,0:T(8,128)(2,1)S(1)}, u32[]{:S(2)}, u32[]{:S(2)}) collective-permute-start(bf16[256,512]{1,0:T(8,128)(2,1)S(1)} %get-tuple-element.166), channel_id=1, source_target_pairs={{0,2},{1,3},{2,0},{3,1},{4,6},{5,7},{6,4},{7,5},{8,10},{9,11},{10,... | collective-permute-start | bytes 786440 | tf_op jit(solution)/shard_map/ppermute | solution.py:17
  238.3 34.0 %collective-permute-start.63 = (bf16[256,512]{1,0:T(8,128)(2,1)S(1)}, bf16[256,512]{1,0:T(8,128)(2,1)S(1)}, u32[]{:S(2)}, u32[]{:S(2)}) collective-permute-start(bf16[256,512]{1,0:T(8,128)(2,1)S(1)} %get-tuple-element.167), channel_id=1, source_target_pairs={{0,2},{1,3},{2,0},{3,1},{4,6},{5,7},{6,4},{7,5},{8,10},{9,11},{10,... | collective-permute-start | bytes 786440 | tf_op jit(solution)/shard_map/ppermute | solution.py:17
  240.0 17.6 %collective-permute-start.60 = (bf16[256,512]{1,0:T(8,128)(2,1)S(1)}, bf16[256,512]{1,0:T(8,128)(2,1)S(1)}, u32[]{:S(2)}, u32[]{:S(2)}) collective-permute-start(bf16[256,512]{1,0:T(8,128)(2,1)S(1)} %multiply_convert_fusion.4), channel_id=1, source_target_pairs={{0,2},{1,3},{2,0},{3,1},{4,6},{5,7},{6,4},{7,5},{8,10},{9,11},{10,... | collective-permute-start | bytes 786440 | tf_op jit(solution)/shard_map/ppermute | solution.py:17
  257.8 15.3 %collective-permute-start.61 = (bf16[256,1024]{1,0:T(8,128)(2,1)S(1)}, bf16[256,1024]{1,0:T(8,128)(2,1)S(1)}, u32[]{:S(2)}, u32[]{:S(2)}) collective-permute-start(bf16[256,1024]{1,0:T(8,128)(2,1)S(1)} %pad_maximum_fusion.13), channel_id=1, source_target_pairs={{0,1},{1,0},{2,3},{3,2},{4,5},{5,4},{6,7},{7,6},{8,9},{9,8},{10,11... | collective-permute-start | bytes 1572872 | tf_op jit(solution)/shard_map/ppermute | solution.py:17
  270.8 14.2 %collective-permute-start.65 = (bf16[256,512]{1,0:T(8,128)(2,1)S(1)}, bf16[256,512]{1,0:T(8,128)(2,1)S(1)}, u32[]{:S(2)}, u32[]{:S(2)}) collective-permute-start(bf16[256,512]{1,0:T(8,128)(2,1)S(1)} %get-tuple-element.177), channel_id=1, source_target_pairs={{0,2},{1,3},{2,0},{3,1},{4,6},{5,7},{6,4},{7,5},{8,10},{9,11},{10,... | collective-permute-start | bytes 786440 | tf_op jit(solution)/shard_map/ppermute | solution.py:17
  272.5 18.1 %collective-permute-start.68 = (bf16[256,512]{1,0:T(8,128)(2,1)S(1)}, bf16[256,512]{1,0:T(8,128)(2,1)S(1)}, u32[]{:S(2)}, u32[]{:S(2)}) collective-permute-start(bf16[256,512]{1,0:T(8,128)(2,1)S(1)} %multiply_convert_fusion.3), channel_id=1, source_target_pairs={{0,2},{1,3},{2,0},{3,1},{4,6},{5,7},{6,4},{7,5},{8,10},{9,11},{10,... | collective-permute-start | bytes 786440 | tf_op jit(solution)/shard_map/ppermute | solution.py:17
  292.4 24.0 %collective-permute-start.46 = (bf16[256,512]{1,0:T(8,128)(2,1)}, bf16[256,512]{1,0:T(8,128)(2,1)}, u32[]{:S(2)}, u32[]{:S(2)}) collective-permute-start(bf16[256,512]{1,0:T(8,128)(2,1)} %get-tuple-element.189), channel_id=1, source_target_pairs={{0,4},{1,5},{2,6},{3,7},{16,20},{17,21},{18,22},{19,23}} | collective-permute-start | bytes 786440 | tf_op jit(solution)/shard_map/ppermute | solution.py:27
  315.0 12.2 %collective-permute-start.49 = (bf16[256,512]{1,0:T(8,128)(2,1)S(1)}, bf16[256,512]{1,0:T(8,128)(2,1)}, u32[]{:S(2)}, u32[]{:S(2)}) collective-permute-start(bf16[256,512]{1,0:T(8,128)(2,1)S(1)} %copy-done.12), channel_id=1, source_target_pairs={{12,8},{13,9},{14,10},{15,11},{28,24},{29,25},{30,26},{31,27}} | collective-permute-start | bytes 786440 | tf_op jit(solution)/shard_map/ppermute | solution.py:27
  333.5 12.3 %collective-permute-start.74 = (bf16[256,512]{1,0:T(8,128)(2,1)}, bf16[256,512]{1,0:T(8,128)(2,1)}, u32[]{:S(2)}, u32[]{:S(2)}) collective-permute-start(bf16[256,512]{1,0:T(8,128)(2,1)} %get-tuple-element.192), channel_id=1, source_target_pairs={{8,4},{9,5},{10,6},{11,7},{12,8},{13,9},{14,10},{15,11},{24,20},{2... | collective-permute-start | bytes 786440 | tf_op jit(solution)/shard_map/ppermute | solution.py:27
  334.9 14.1 %collective-permute-start.48 = (bf16[256,512]{1,0:T(8,128)(2,1)}, bf16[256,512]{1,0:T(8,128)(2,1)S(1)}, u32[]{:S(2)}, u32[]{:S(2)}) collective-permute-start(bf16[256,512]{1,0:T(8,128)(2,1)} %get-tuple-element.187), channel_id=1, source_target_pairs={{0,4},{1,5},{2,6},{3,7},{4,8},{5,9},{6,10},{7,11},{8,12},{9,13},{1... | collective-permute-start | bytes 786440 | tf_op jit(solution)/shard_map/ppermute | solution.py:27
  (41 other events, 524.7 us)
where the time goes:
time: 360 us; the launch traced here: 358 us
  Pallas kernels  146 us (41%)
  starting transfers between devices  101 us (28%)
  waiting for transfers between devices  83.4 us (23%)
  other arithmetic  19.9 us (6%)
  local copies, waits for them, and re-layouts  6.73 us (2%)
    ppermute x24, starting transfers between devices, shift(): return lax.ppermute(block, 'wide', route)  66.6 us
    ppermute x52, waiting for transfers between devices, partner(): lax.ppermute(block, 'wide', [(i, i ^ 1 << bit) for i in range(count)])  59.3 us
    pallas_call x8, Pallas kernels, project_near(): pl.pallas_call(lambda *refs: near_kernel(n, *refs), grid_spec=pltpu.Prefe...  51.6 us
    pallas_call x8, Pallas kernels, project_away(): pl.pallas_call(away_kernel, grid_spec=pltpu.PrefetchScalarGridSpec(num_sc...  49.2 us
    pallas_call x8, Pallas kernels, project_down(): pl.pallas_call(down_kernel, grid=(width // tile,), in_specs=[pl.BlockSpec...  45.5 us
    ppermute x52, starting transfers between devices, partner(): lax.ppermute(block, 'wide', [(i, i ^ 1 << bit) for i in range(count)])  34 us
    ppermute x24, waiting for transfers between devices, shift(): return lax.ppermute(block, 'wide', route)  24.1 us
  transfers between devices with their start and end apart: 76, of which 19 were waited for; matrix products, arithmetic and copies ran while one was open for 5% of the time, Pallas kernels for 39%

commit v1 on v0

--- a/solution.py
+++ b/solution.py
@@ -6,8 +6,8 @@
 from jax.sharding import PartitionSpec as P
 
 WSPLIT = 4
-ROW_CHUNKS = 2
-UNIT_CHUNKS = 4
+ROW_CHUNKS = 1
+UNIT_CHUNKS = 8
 
 epsilon = 1e-05
 

time: 360 us -> 349 us (0.969)
  waiting for transfers between devices: 83.4 us -> 121 us
  starting transfers between devices: 101 us -> 72 us
  Pallas kernels: 146 us -> 120 us
  other arithmetic: 19.9 us -> 25 us
    ppermute x24 -> x12, starting transfers between devices: 66.6 us -> 32.9 us  [shift(): return lax.ppermute(block, 'wide', route)]
    ppermute x24 -> x12, waiting for transfers between devices: 24.1 us -> 55.3 us  [shift(): return lax.ppermute(block, 'wide', route)]
    pallas_call x8, Pallas kernels: 51.6 us -> 39.2 us  [project_near(): pl.pallas_call(lambda *refs: near_kernel(n, *refs), grid_spec=pltpu.Prefe...]
    pallas_call x8, Pallas kernels: 49.2 us -> 40.4 us  [project_away(): pl.pallas_call(away_kernel, grid_spec=pltpu.PrefetchScalarGridSpec(num_sc...]
    ppermute x52, waiting for transfers between devices: 59.3 us -> 66 us  [partner(): lax.ppermute(block, 'wide', [(i, i ^ 1 << bit) for i in range(count)])]
    pallas_call x8, Pallas kernels: 45.5 us -> 40.1 us  [project_down(): pl.pallas_call(down_kernel, grid=(width // tile,), in_specs=[pl.BlockSpec...]
    ppermute x52, starting transfers between devices: 34 us -> 39.1 us  [partner(): lax.ppermute(block, 'wide', [(i, i ^ 1 << bit) for i in range(count)])]
    unnamed x26 -> x42, local copies, waits for them, and re-layouts: 3.61 us -> 7.41 us
  transfers between devices with their start and end apart: 76 -> 64, of which waited for: 19 -> 19; matrix products, arithmetic and copies ran while one was open for 5% -> 5% of each run, Pallas kernels for 39% -> 31%
where the time goes in v1:
time: 349 us; the launch traced here: 348 us
  waiting for transfers between devices  121 us (35%)
  Pallas kernels  120 us (34%)
  starting transfers between devices  72 us (21%)
  other arithmetic  25 us (7%)
  local copies, waits for them, and re-layouts  8.66 us (2%)
    ppermute x52, waiting for transfers between devices, partner(): lax.ppermute(block, 'wide', [(i, i ^ 1 << bit) for i in range(count)])  66 us
    ppermute x12, waiting for transfers between devices, shift(): return lax.ppermute(block, 'wide', route)  55.3 us
    pallas_call x8, Pallas kernels, project_away(): pl.pallas_call(away_kernel, grid_spec=pltpu.PrefetchScalarGridSpec(num_sc...  40.4 us
    pallas_call x8, Pallas kernels, project_down(): pl.pallas_call(down_kernel, grid=(width // tile,), in_specs=[pl.BlockSpec...  40.1 us
    pallas_call x8, Pallas kernels, project_near(): pl.pallas_call(lambda *refs: near_kernel(n, *refs), grid_spec=pltpu.Prefe...  39.2 us
    ppermute x52, starting transfers between devices, partner(): lax.ppermute(block, 'wide', [(i, i ^ 1 << bit) for i in range(count)])  39.1 us
    ppermute x12, starting transfers between devices, shift(): return lax.ppermute(block, 'wide', route)  32.9 us
    unnamed x42, local copies, waits for them, and re-layouts  7.41 us
  transfers between devices with their start and end apart: 64, of which 19 were waited for; matrix products, arithmetic and copies ran while one was open for 5% of the time, Pallas kernels for 31%

profile of v1, /device:TPU:0, one launch (start us, length us, event | category | flops | bytes accessed | tf_op | source)
XLA Modules:
  0.0 347.8 jit_solution(16967401524516896712)
XLA Ops:
  0.0 5.1 %collective-permute-start.3 = (bf16[512,512]{1,0:T(8,128)(2,1)}, bf16[512,512]{1,0:T(8,128)(2,1)S(1)}, u32[]{:S(2)}, u32[]{:S(2)}) collective-permute-start(bf16[512,512]{1,0:T(8,128)(2,1)} %param.5), channel_id=1, source_target_pairs={{0,4},{1,5},{2,6},{3,7},{4,8},{5,9},{6,10},{7,11},{8,12},{9,13},{1... | collective-permute-start | bytes 1572872 | tf_op jit(solution)/shard_map/ppermute | solution.py:27
  7.8 8.7 %collective-permute-done.3 = bf16[512,512]{1,0:T(8,128)(2,1)S(1)} collective-permute-done((bf16[512,512]{1,0:T(8,128)(2,1)}, bf16[512,512]{1,0:T(8,128)(2,1)S(1)}, u32[]{:S(2)}, u32[]{:S(2)}) %collective-permute-start.3) | collective-permute-done | bytes 524320 | tf_op jit(solution)/shard_map/ppermute | solution.py:27
  16.5 5.1 %collective-permute-start.4 = (bf16[512,512]{1,0:T(8,128)(2,1)S(1)}, bf16[512,512]{1,0:T(8,128)(2,1)}, u32[]{:S(2)}, u32[]{:S(2)}) collective-permute-start(bf16[512,512]{1,0:T(8,128)(2,1)S(1)} %collective-permute-done.3), channel_id=1, source_target_pairs={{0,4},{1,5},{2,6},{3,7},{4,8},{5,9},{6,10},{7,11},{8,12},{9,13},{1... | collective-permute-start | bytes 1572872 | tf_op jit(solution)/shard_map/ppermute | solution.py:27
  25.6 5.6 %collective-permute-done.4 = bf16[512,512]{1,0:T(8,128)(2,1)} collective-permute-done((bf16[512,512]{1,0:T(8,128)(2,1)S(1)}, bf16[512,512]{1,0:T(8,128)(2,1)}, u32[]{:S(2)}, u32[]{:S(2)}) %collective-permute-start.4) | collective-permute-done | bytes 524320 | tf_op jit(solution)/shard_map/ppermute | solution.py:27
  31.2 5.3 %collective-permute-start.5 = (bf16[512,512]{1,0:T(8,128)(2,1)}, bf16[512,512]{1,0:T(8,128)(2,1)}, u32[]{:S(2)}, u32[]{:S(2)}) collective-permute-start(bf16[512,512]{1,0:T(8,128)(2,1)} %collective-permute-done.4), channel_id=1, source_target_pairs={{0,4},{1,5},{2,6},{3,7},{4,8},{5,9},{6,10},{7,11},{8,12},{9,13},{1... | collective-permute-start | bytes 1572872 | tf_op jit(solution)/shard_map/ppermute | solution.py:27
  37.8 2.7 collective-permute-start.8
  40.6 9.9 %collective-permute-done.8 = f32[512]{0:T(512)S(1)} collective-permute-done((f32[512]{0:T(512)S(1)}, f32[512]{0:T(512)S(1)}, u32[]{:S(2)}, u32[]{:S(2)}) %collective-permute-start.8) | collective-permute-done | bytes 2080 | tf_op jit(solution)/shard_map/ppermute | solution.py:17
  52.1 2.9 collective-permute-done.9
  54.9 3.2 select_select_fusion
  59.2 5.5 %shard_map.55 = (bf16[512,512]{1,0:T(8,128)(2,1)}, bf16[512,512]{1,0:T(8,128)(2,1)}) custom-call(s32[2]{0:T(128)S(1)} %iota_add_fusion.4.order, bf16[512,2048]{1,0:T(8,128)(2,1)S(1)} %multiply_convert_fusion.a.refs_2_, bf16[1,2048,8192]{2,1,0:T(8,128)(2,1)} %refs_3_.15, bf16[1,2048,8192]{2,1,0:T(8,128)(2,1)} %refs_4_.15), custom_call_target="tpu_custom_call" | custom-call | flops 2147483648 | bytes 4194304 | tf_op jit(solution)/shard_map/pallas_call | solution.py:92
  65.2 5.5 %shard_map.56 = (bf16[512,512]{1,0:T(8,128)(2,1)}, bf16[512,512]{1,0:T(8,128)(2,1)}) custom-call(s32[2]{0:T(128)S(1)} %iota_add_fusion.5.order, bf16[512,2048]{1,0:T(8,128)(2,1)S(1)} %multiply_convert_fusion.a.refs_2_, bf16[1,2048,8192]{2,1,0:T(8,128)(2,1)} %refs_3_.15, bf16[1,2048,8192]{2,1,0:T(8,128)(2,1)} %refs_4_.15), custom_call_target="tpu_custom_call" | custom-call | flops 2147483648 | bytes 4194304 | tf_op jit(solution)/shard_map/pallas_call | solution.py:92
  71.2 5.0 %shard_map.57 = (bf16[512,256]{1,0:T(8,128)(2,1)S(1)}, bf16[512,256]{1,0:T(8,128)(2,1)S(1)}, f32[512,256]{1,0:T(8,128)S(1)}, f32[512,256]{1,0:T(8,128)S(1)}) custom-call(s32[2]{0:T(128)S(1)} %get-tuple-element.228.refs_0_, s32[2]{0:T(128)S(1)} %get-tuple-element.184.refs_1_, bf16[512,2048]{1,0:T(8,128)(2,1)S(1)} %multiply_convert_fusion.a.refs_2_, ...), custom_call_target="tpu_custom_call" | custom-call | flops 2147483648 | bytes 4194304 | tf_op jit(solution)/shard_map/pallas_call | solution.py:128
  78.3 4.7 %shard_map.58 = (bf16[512,512]{1,0:T(8,128)(2,1)S(1)}, bf16[512,512]{1,0:T(8,128)(2,1)S(1)}) custom-call(s32[2]{0:T(128)S(1)} %iota_add_fusion.6.order, bf16[512,2048]{1,0:T(8,128)(2,1)S(1)} %multiply_convert_fusion.a.refs_2_, bf16[1,2048,8192]{2,1,0:T(8,128)(2,1)} %refs_3_.15, bf16[1,2048,8192]{2,1,0:T(8,128)(2,1)} %refs_4_.15), custom_call_target="tpu_custom_call" | custom-call | flops 2147483648 | bytes 4194304 | tf_op jit(solution)/shard_map/pallas_call | solution.py:92
  83.7 4.8 %shard_map.59 = (bf16[512,256]{1,0:T(8,128)(2,1)S(1)}, bf16[512,256]{1,0:T(8,128)(2,1)S(1)}, f32[512,256]{1,0:T(8,128)S(1)}, f32[512,256]{1,0:T(8,128)S(1)}) custom-call(s32[2]{0:T(128)S(1)} %get-tuple-element.229.refs_0_, s32[2]{0:T(128)S(1)} %get-tuple-element.184.refs_1_, bf16[512,2048]{1,0:T(8,128)(2,1)S(1)} %multiply_convert_fusion.a.refs_2_, ...), custom_call_target="tpu_custom_call" | custom-call | flops 2147483648 | bytes 4194304 | tf_op jit(solution)/shard_map/pallas_call | solution.py:128
  94.0 4.7 %shard_map.60 = (bf16[512,512]{1,0:T(8,128)(2,1)S(1)}, bf16[512,512]{1,0:T(8,128)(2,1)S(1)}) custom-call(s32[2]{0:T(128)S(1)} %iota_add_fusion.3.order, bf16[512,2048]{1,0:T(8,128)(2,1)S(1)} %multiply_convert_fusion.a.refs_2_, bf16[1,2048,8192]{2,1,0:T(8,128)(2,1)} %refs_3_.15, bf16[1,2048,8192]{2,1,0:T(8,128)(2,1)} %refs_4_.15), custom_call_target="tpu_custom_call" | custom-call | flops 2147483648 | bytes 4194304 | tf_op jit(solution)/shard_map/pallas_call | solution.py:92
  99.8 4.8 %shard_map.61 = (bf16[512,256]{1,0:T(8,128)(2,1)S(1)}, bf16[512,256]{1,0:T(8,128)(2,1)S(1)}, f32[512,256]{1,0:T(8,128)S(1)}, f32[512,256]{1,0:T(8,128)S(1)}) custom-call(s32[2]{0:T(128)S(1)} %get-tuple-element.227.refs_0_, s32[2]{0:T(128)S(1)} %get-tuple-element.184.refs_1_, bf16[512,2048]{1,0:T(8,128)(2,1)S(1)} %multiply_convert_fusion.a.refs_2_, ...), custom_call_target="tpu_custom_call" | custom-call | flops 2147483648 | bytes 4194304 | tf_op jit(solution)/shard_map/pallas_call | solution.py:128
  105.3 3.8 %collective-permute-done.19 = bf16[512,256]{1,0:T(8,128)(2,1)S(1)} collective-permute-done((bf16[512,256]{1,0:T(8,128)(2,1)S(1)}, bf16[512,256]{1,0:T(8,128)(2,1)S(1)}, u32[]{:S(2)}, u32[]{:S(2)}) %collective-permute-start.19) | collective-permute-done | bytes 262176 | tf_op jit(solution)/shard_map/ppermute | solution.py:17
  113.5 3.6 %collective-permute-done.20 = bf16[512,256]{1,0:T(8,128)(2,1)} collective-permute-done((bf16[512,256]{1,0:T(8,128)(2,1)}, bf16[512,256]{1,0:T(8,128)(2,1)}, u32[]{:S(2)}, u32[]{:S(2)}) %collective-permute-start.20) | collective-permute-done | bytes 262176 | tf_op jit(solution)/shard_map/ppermute | solution.py:17
  117.1 2.5 collective-permute-start.27
  122.2 4.9 %shard_map.62.refs_0_ = f32[512,2048]{1,0:T(8,128)S(1)} custom-call(bf16[512,1024]{1,0:T(8,128)(2,1)S(1)} %pad_maximum_fusion.1.a, bf16[1,8192,2048]{2,1,0:T(8,128)(2,1)} %weight.15), custom_call_target="tpu_custom_call" | custom-call | flops 2147483648 | bytes 4194304 | tf_op jit(solution)/shard_map/pallas_call | solution.py:157
  127.1 4.8 %shard_map.63 = (bf16[512,512]{1,0:T(8,128)(2,1)S(1)}, bf16[512,512]{1,0:T(8,128)(2,1)S(1)}) custom-call(s32[2]{0:T(128)S(1)} %iota_add_fusion.2.order, bf16[512,2048]{1,0:T(8,128)(2,1)S(1)} %multiply_convert_fusion.a.refs_2_, bf16[1,2048,8192]{2,1,0:T(8,128)(2,1)} %refs_3_.15, bf16[1,2048,8192]{2,1,0:T(8,128)(2,1)} %refs_4_.15), custom_call_target="tpu_custom_call" | custom-call | flops 2147483648 | bytes 4194304 | tf_op jit(solution)/shard_map/pallas_call | solution.py:92
  131.8 5.1 %shard_map.64 = (bf16[512,256]{1,0:T(8,128)(2,1)S(1)}, bf16[512,256]{1,0:T(8,128)(2,1)S(1)}, f32[512,256]{1,0:T(8,128)S(1)}, f32[512,256]{1,0:T(8,128)S(1)}) custom-call(s32[2]{0:T(128)S(1)} %get-tuple-element.226.refs_0_, s32[2]{0:T(128)S(1)} %get-tuple-element.184.refs_1_, bf16[512,2048]{1,0:T(8,128)(2,1)S(1)} %multiply_convert_fusion.a.refs_2_, ...), custom_call_target="tpu_custom_call" | custom-call | flops 2147483648 | bytes 4194304 | tf_op jit(solution)/shard_map/pallas_call | solution.py:128
  140.3 5.0 %shard_map.65.refs_0_ = f32[512,2048]{1,0:T(8,128)S(1)} custom-call(bf16[512,1024]{1,0:T(8,128)(2,1)S(1)} %pad_maximum_fusion.a, bf16[1,8192,2048]{2,1,0:T(8,128)(2,1)} %weight.15, f32[512,2048]{1,0:T(8,128)S(1)} %shard_map.62.refs_0_), custom_call_target="tpu_custom_call" | custom-call | flops 2147483648 | bytes 4194304 | tf_op jit(solution)/shard_map/pallas_call | solution.py:157
  145.3 11.7 %collective-permute-done.30 = bf16[512,256]{1,0:T(8,128)(2,1)S(1)} collective-permute-done((bf16[512,256]{1,0:T(8,128)(2,1)S(1)}, bf16[512,256]{1,0:T(8,128)(2,1)S(1)}, u32[]{:S(2)}, u32[]{:S(2)}) %collective-permute-start.30) | collective-permute-done | bytes 262176 | tf_op jit(solution)/shard_map/ppermute | solution.py:17
  157.1 4.8 %shard_map.66 = (bf16[512,512]{1,0:T(8,128)(2,1)S(1)}, bf16[512,512]{1,0:T(8,128)(2,1)S(1)}) custom-call(s32[2]{0:T(128)S(1)} %iota_add_fusion.7.order, bf16[512,2048]{1,0:T(8,128)(2,1)S(1)} %multiply_convert_fusion.a.refs_2_, bf16[1,2048,8192]{2,1,0:T(8,128)(2,1)} %refs_3_.15, bf16[1,2048,8192]{2,1,0:T(8,128)(2,1)} %refs_4_.15), custom_call_target="tpu_custom_call" | custom-call | flops 2147483648 | bytes 4194304 | tf_op jit(solution)/shard_map/pallas_call | solution.py:92
  162.5 4.8 %shard_map.67 = (bf16[512,256]{1,0:T(8,128)(2,1)S(1)}, bf16[512,256]{1,0:T(8,128)(2,1)S(1)}, f32[512,256]{1,0:T(8,128)S(1)}, f32[512,256]{1,0:T(8,128)S(1)}) custom-call(s32[2]{0:T(128)S(1)} %get-tuple-element.230.refs_0_, s32[2]{0:T(128)S(1)} %get-tuple-element.184.refs_1_, bf16[512,2048]{1,0:T(8,128)(2,1)S(1)} %multiply_convert_fusion.a.refs_2_, ...), custom_call_target="tpu_custom_call" | custom-call | flops 2147483648 | bytes 4194304 | tf_op jit(solution)/shard_map/pallas_call | solution.py:128
  170.4 5.0 %shard_map.68.refs_0_ = f32[512,2048]{1,0:T(8,128)S(1)} custom-call(bf16[512,1024]{1,0:T(8,128)(2,1)S(1)} %pad_maximum_fusion.2.a, bf16[1,8192,2048]{2,1,0:T(8,128)(2,1)} %weight.15, f32[512,2048]{1,0:T(8,128)S(1)} %shard_map.65.refs_0_), custom_call_target="tpu_custom_call" | custom-call | flops 2147483648 | bytes 4194304 | tf_op jit(solution)/shard_map/pallas_call | solution.py:157
  175.4 5.7 %shard_map.69 = (bf16[512,512]{1,0:T(8,128)(2,1)S(1)}, bf16[512,512]{1,0:T(8,128)(2,1)S(1)}) custom-call(s32[2]{0:T(128)S(1)} %iota_add_fusion.1.order, bf16[512,2048]{1,0:T(8,128)(2,1)S(1)} %multiply_convert_fusion.a.refs_2_, bf16[1,2048,8192]{2,1,0:T(8,128)(2,1)} %refs_3_.15, bf16[1,2048,8192]{2,1,0:T(8,128)(2,1)} %refs_4_.15), custom_call_target="tpu_custom_call" | custom-call | flops 2147483648 | bytes 4194304 | tf_op jit(solution)/shard_map/pallas_call | solution.py:92
  181.9 4.8 %shard_map.70 = (bf16[512,256]{1,0:T(8,128)(2,1)S(1)}, bf16[512,256]{1,0:T(8,128)(2,1)S(1)}, f32[512,256]{1,0:T(8,128)S(1)}, f32[512,256]{1,0:T(8,128)S(1)}) custom-call(s32[2]{0:T(128)S(1)} %get-tuple-element.225.refs_0_, s32[2]{0:T(128)S(1)} %get-tuple-element.184.refs_1_, bf16[512,2048]{1,0:T(8,128)(2,1)S(1)} %multiply_convert_fusion.a.refs_2_, ...), custom_call_target="tpu_custom_call" | custom-call | flops 2147483648 | bytes 4194304 | tf_op jit(solution)/shard_map/pallas_call | solution.py:128
  193.2 4.0 %collective-permute-done.38 = bf16[512,256]{1,0:T(8,128)(2,1)} collective-permute-done((bf16[512,256]{1,0:T(8,128)(2,1)}, bf16[512,256]{1,0:T(8,128)(2,1)}, u32[]{:S(2)}, u32[]{:S(2)}) %collective-permute-start.38) | collective-permute-done | bytes 262176 | tf_op jit(solution)/shard_map/ppermute | solution.py:17
  200.7 5.0 %shard_map.71.refs_0_ = f32[512,2048]{1,0:T(8,128)S(1)} custom-call(bf16[512,1024]{1,0:T(8,128)(2,1)S(1)} %pad_maximum_fusion.4.a, bf16[1,8192,2048]{2,1,0:T(8,128)(2,1)} %weight.15, f32[512,2048]{1,0:T(8,128)S(1)} %copy-done.2), custom_call_target="tpu_custom_call" | custom-call | flops 2147483648 | bytes 4194304 | tf_op jit(solution)/shard_map/pallas_call | solution.py:157
  205.7 4.8 %shard_map.72 = (bf16[512,512]{1,0:T(8,128)(2,1)S(1)}, bf16[512,512]{1,0:T(8,128)(2,1)S(1)}) custom-call(s32[2]{0:T(128)S(1)} %iota_add_fusion.order, bf16[512,2048]{1,0:T(8,128)(2,1)S(1)} %multiply_convert_fusion.a.refs_2_, bf16[1,2048,8192]{2,1,0:T(8,128)(2,1)} %refs_3_.15, bf16[1,2048,8192]{2,1,0:T(8,128)(2,1)} %refs_4_.15), custom_call_target="tpu_custom_call" | custom-call | flops 2147483648 | bytes 4194304 | tf_op jit(solution)/shard_map/pallas_call | solution.py:92
  210.5 4.8 %shard_map.73 = (bf16[512,256]{1,0:T(8,128)(2,1)S(1)}, bf16[512,256]{1,0:T(8,128)(2,1)S(1)}, f32[512,256]{1,0:T(8,128)S(1)}, f32[512,256]{1,0:T(8,128)S(1)}) custom-call(s32[2]{0:T(128)S(1)} %get-tuple-element.183.refs_0_, s32[2]{0:T(128)S(1)} %get-tuple-element.184.refs_1_, bf16[512,2048]{1,0:T(8,128)(2,1)S(1)} %multiply_convert_fusion.a.refs_2_, ...), custom_call_target="tpu_custom_call" | custom-call | flops 2147483648 | bytes 4194304 | tf_op jit(solution)/shard_map/pallas_call | solution.py:128
  220.4 15.0 %collective-permute-done.48 = bf16[512,256]{1,0:T(8,128)(2,1)S(1)} collective-permute-done((bf16[512,256]{1,0:T(8,128)(2,1)S(1)}, bf16[512,256]{1,0:T(8,128)(2,1)S(1)}, u32[]{:S(2)}, u32[]{:S(2)}) %collective-permute-start.48) | collective-permute-done | bytes 262176 | tf_op jit(solution)/shard_map/ppermute | solution.py:17
  235.6 5.2 %shard_map.74.refs_0_ = f32[512,2048]{1,0:T(8,128)S(1)} custom-call(bf16[512,1024]{1,0:T(8,128)(2,1)S(1)} %pad_maximum_fusion.3.a, bf16[1,8192,2048]{2,1,0:T(8,128)(2,1)} %weight.15, f32[512,2048]{1,0:T(8,128)S(1)} %shard_map.71.refs_0_), custom_call_target="tpu_custom_call" | custom-call | flops 2147483648 | bytes 4194304 | tf_op jit(solution)/shard_map/pallas_call | solution.py:157
  240.8 4.8 %shard_map.75 = (bf16[512,256]{1,0:T(8,128)(2,1)S(1)}, bf16[512,256]{1,0:T(8,128)(2,1)S(1)}, f32[512,256]{1,0:T(8,128)S(1)}, f32[512,256]{1,0:T(8,128)S(1)}) custom-call(s32[2]{0:T(128)S(1)} %get-tuple-element.231.refs_0_, s32[2]{0:T(128)S(1)} %get-tuple-element.184.refs_1_, bf16[512,2048]{1,0:T(8,128)(2,1)S(1)} %multiply_convert_fusion.a.refs_2_, ...), custom_call_target="tpu_custom_call" | custom-call | flops 2147483648 | bytes 4194304 | tf_op jit(solution)/shard_map/pallas_call | solution.py:128
  250.2 5.0 %shard_map.76.refs_0_ = f32[512,2048]{1,0:T(8,128)S(1)} custom-call(bf16[512,1024]{1,0:T(8,128)(2,1)S(1)} %pad_maximum_fusion.5.a, bf16[1,8192,2048]{2,1,0:T(8,128)(2,1)} %weight.15, f32[512,2048]{1,0:T(8,128)S(1)} %shard_map.74.refs_0_), custom_call_target="tpu_custom_call" | custom-call | flops 2147483648 | bytes 4194304 | tf_op jit(solution)/shard_map/pallas_call | solution.py:157
  257.2 3.3 collective-permute-done.53
  262.5 3.6 %collective-permute-done.56 = bf16[512,256]{1,0:T(8,128)(2,1)S(1)} collective-permute-done((bf16[512,256]{1,0:T(8,128)(2,1)S(1)}, bf16[512,256]{1,0:T(8,128)(2,1)S(1)}, u32[]{:S(2)}, u32[]{:S(2)}) %collective-permute-start.56) | collective-permute-done | bytes 262176 | tf_op jit(solution)/shard_map/ppermute | solution.py:17
  266.3 5.0 %collective-permute-done.54 = bf16[512,256]{1,0:T(8,128)(2,1)S(1)} collective-permute-done((bf16[512,256]{1,0:T(8,128)(2,1)S(1)}, bf16[512,256]{1,0:T(8,128)(2,1)S(1)}, u32[]{:S(2)}, u32[]{:S(2)}) %collective-permute-start.54) | collective-permute-done | bytes 262176 | tf_op jit(solution)/shard_map/ppermute | solution.py:17
  273.6 5.0 %shard_map.77.refs_0_ = f32[512,2048]{1,0:T(8,128)S(1)} custom-call(bf16[512,1024]{1,0:T(8,128)(2,1)S(1)} %pad_maximum_fusion.7.a, bf16[1,8192,2048]{2,1,0:T(8,128)(2,1)} %weight.15, f32[512,2048]{1,0:T(8,128)S(1)} %copy-done.4), custom_call_target="tpu_custom_call" | custom-call | flops 2147483648 | bytes 4194304 | tf_op jit(solution)/shard_map/pallas_call | solution.py:157
  278.9 5.0 %shard_map.78 = f32[512,2048]{1,0:T(8,128)S(1)} custom-call(bf16[512,1024]{1,0:T(8,128)(2,1)S(1)} %pad_maximum_fusion.6.a, bf16[1,8192,2048]{2,1,0:T(8,128)(2,1)} %weight.15, f32[512,2048]{1,0:T(8,128)S(1)} %shard_map.77.refs_0_), custom_call_target="tpu_custom_call" | custom-call | flops 2147483648 | bytes 4194304 | tf_op jit(solution)/shard_map/pallas_call | solution.py:157
  288.3 10.4 %collective-permute-done.58 = bf16[512,512]{1,0:T(8,128)(2,1)S(1)} collective-permute-done((bf16[512,512]{1,0:T(8,128)(2,1)S(1)}, bf16[512,512]{1,0:T(8,128)(2,1)S(1)}, u32[]{:S(2)}, u32[]{:S(2)}) %collective-permute-start.58) | collective-permute-done | bytes 524320 | tf_op jit(solution)/shard_map/ppermute | solution.py:27
  300.1 4.4 %collective-permute-start.59 = (bf16[512,512]{1,0:T(8,128)(2,1)S(1)}, bf16[512,512]{1,0:T(8,128)(2,1)S(1)}, u32[]{:S(2)}, u32[]{:S(2)}) collective-permute-start(bf16[512,512]{1,0:T(8,128)(2,1)S(1)} %add_convert_fusion.4), channel_id=1, source_target_pairs={{0,4},{1,5},{2,6},{3,7},{4,8},{5,9},{6,10},{7,11},{16,20},{17,21},... | collective-permute-start | bytes 1572872 | tf_op jit(solution)/shard_map/ppermute | solution.py:27
  304.6 10.2 %collective-permute-done.59 = bf16[512,512]{1,0:T(8,128)(2,1)S(1)} collective-permute-done((bf16[512,512]{1,0:T(8,128)(2,1)S(1)}, bf16[512,512]{1,0:T(8,128)(2,1)S(1)}, u32[]{:S(2)}, u32[]{:S(2)}) %collective-permute-start.59) | collective-permute-done | bytes 524320 | tf_op jit(solution)/shard_map/ppermute | solution.py:27
  317.5 5.0 %collective-permute-start.60 = (bf16[512,512]{1,0:T(8,128)(2,1)S(1)}, bf16[512,512]{1,0:T(8,128)(2,1)S(1)}, u32[]{:S(2)}, u32[]{:S(2)}) collective-permute-start(bf16[512,512]{1,0:T(8,128)(2,1)S(1)} %get-tuple-element.185), channel_id=1, source_target_pairs={{0,4},{1,5},{2,6},{3,7},{4,8},{5,9},{6,10},{7,11},{8,12},{9,13},{1... | collective-permute-start | bytes 1572872 | tf_op jit(solution)/shard_map/ppermute | solution.py:27
  325.3 6.6 %collective-permute-done.60 = bf16[512,512]{1,0:T(8,128)(2,1)S(1)} collective-permute-done((bf16[512,512]{1,0:T(8,128)(2,1)S(1)}, bf16[512,512]{1,0:T(8,128)(2,1)S(1)}, u32[]{:S(2)}, u32[]{:S(2)}) %collective-permute-start.60) | collective-permute-done | bytes 524320 | tf_op jit(solution)/shard_map/ppermute | solution.py:27
  331.9 13.7 %collective-permute-done.63 = bf16[512,512]{1,0:T(8,128)(2,1)S(1)} collective-permute-done((bf16[512,512]{1,0:T(8,128)(2,1)S(1)}, bf16[512,512]{1,0:T(8,128)(2,1)S(1)}, u32[]{:S(2)}, u32[]{:S(2)}) %collective-permute-start.63) | collective-permute-done | bytes 524320 | tf_op jit(solution)/shard_map/ppermute | solution.py:27
  (216 shorter events, 75.7 us)
Async XLA Ops:
  0.0 16.5 %collective-permute-start.3 = (bf16[512,512]{1,0:T(8,128)(2,1)}, bf16[512,512]{1,0:T(8,128)(2,1)S(1)}, u32[]{:S(2)}, u32[]{:S(2)}) collective-permute-start(bf16[512,512]{1,0:T(8,128)(2,1)} %param.5), channel_id=1, source_target_pairs={{0,4},{1,5},{2,6},{3,7},{4,8},{5,9},{6,10},{7,11},{8,12},{9,13},{1... | collective-permute-start | bytes 1572872 | tf_op jit(solution)/shard_map/ppermute | solution.py:27
  5.1 16.5 %collective-permute-start = (bf16[512,512]{1,0:T(8,128)(2,1)}, bf16[512,512]{1,0:T(8,128)(2,1)}, u32[]{:S(2)}, u32[]{:S(2)}) collective-permute-start(bf16[512,512]{1,0:T(8,128)(2,1)} %param.5), channel_id=1, source_target_pairs={{4,0},{5,1},{6,2},{7,3},{8,4},{9,5},{10,6},{11,7},{12,8},{13,9},{1... | collective-permute-start | bytes 1572872 | tf_op jit(solution)/shard_map/ppermute | solution.py:27
  7.6 16.4 %collective-permute-start.6 = (f32[512]{0:T(512)S(1)}, f32[512]{0:T(512)S(1)}, u32[]{:S(2)}, u32[]{:S(2)}) collective-permute-start(f32[512]{0:T(512)S(1)} %multiply_reduce_fusion), channel_id=1, source_target_pairs={{0,1},{1,0},{2,3},{3,2},{4,5},{5,4},{6,7},{7,6},{8,9},{9,8},{10,11... | collective-permute-start | bytes 6152 | tf_op jit(solution)/shard_map/ppermute | solution.py:17
  16.5 14.7 %collective-permute-start.4 = (bf16[512,512]{1,0:T(8,128)(2,1)S(1)}, bf16[512,512]{1,0:T(8,128)(2,1)}, u32[]{:S(2)}, u32[]{:S(2)}) collective-permute-start(bf16[512,512]{1,0:T(8,128)(2,1)S(1)} %collective-permute-done.3), channel_id=1, source_target_pairs={{0,4},{1,5},{2,6},{3,7},{4,8},{5,9},{6,10},{7,11},{8,12},{9,13},{1... | collective-permute-start | bytes 1572872 | tf_op jit(solution)/shard_map/ppermute | solution.py:27
  21.6 14.9 %collective-permute-start.1 = (bf16[512,512]{1,0:T(8,128)(2,1)}, bf16[512,512]{1,0:T(8,128)(2,1)}, u32[]{:S(2)}, u32[]{:S(2)}) collective-permute-start(bf16[512,512]{1,0:T(8,128)(2,1)} %collective-permute-done), channel_id=1, source_target_pairs={{4,0},{5,1},{6,2},{7,3},{8,4},{9,5},{10,6},{11,7},{12,8},{13,9},{1... | collective-permute-start | bytes 1572872 | tf_op jit(solution)/shard_map/ppermute | solution.py:27
  24.0 13.8 %collective-permute-start.7 = (f32[512]{0:T(512)S(1)}, f32[512]{0:T(512)S(1)}, u32[]{:S(2)}, u32[]{:S(2)}) collective-permute-start(f32[512]{0:T(512)S(1)} %add.354), channel_id=1, source_target_pairs={{0,2},{1,3},{2,0},{3,1},{4,6},{5,7},{6,4},{7,5},{8,10},{9,11},{10,... | collective-permute-start | bytes 6152 | tf_op jit(solution)/shard_map/ppermute | solution.py:17
  31.2 23.7 %collective-permute-start.5 = (bf16[512,512]{1,0:T(8,128)(2,1)}, bf16[512,512]{1,0:T(8,128)(2,1)}, u32[]{:S(2)}, u32[]{:S(2)}) collective-permute-start(bf16[512,512]{1,0:T(8,128)(2,1)} %collective-permute-done.4), channel_id=1, source_target_pairs={{0,4},{1,5},{2,6},{3,7},{4,8},{5,9},{6,10},{7,11},{8,12},{9,13},{1... | collective-permute-start | bytes 1572872 | tf_op jit(solution)/shard_map/ppermute | solution.py:27
  36.5 18.4 %collective-permute-start.2 = (bf16[512,512]{1,0:T(8,128)(2,1)}, bf16[512,512]{1,0:T(8,128)(2,1)}, u32[]{:S(2)}, u32[]{:S(2)}) collective-permute-start(bf16[512,512]{1,0:T(8,128)(2,1)} %collective-permute-done.1), channel_id=1, source_target_pairs={{4,0},{5,1},{6,2},{7,3},{8,4},{9,5},{10,6},{11,7},{12,8},{13,9},{1... | collective-permute-start | bytes 1572872 | tf_op jit(solution)/shard_map/ppermute | solution.py:27
  37.8 12.6 %collective-permute-start.8 = (f32[512]{0:T(512)S(1)}, f32[512]{0:T(512)S(1)}, u32[]{:S(2)}, u32[]{:S(2)}) collective-permute-start(f32[512]{0:T(512)S(1)} %add.355), channel_id=1, source_target_pairs={{0,4},{1,5},{2,6},{3,7},{4,0},{5,1},{6,2},{7,3},{8,12},{9,13},{10,... | collective-permute-start | bytes 6152 | tf_op jit(solution)/shard_map/ppermute | solution.py:17
  70.7 13.0 %collective-permute-start.13 = (bf16[512,512]{1,0:T(8,128)(2,1)}, bf16[512,512]{1,0:T(8,128)(2,1)S(1)}, u32[]{:S(2)}, u32[]{:S(2)}) collective-permute-start(bf16[512,512]{1,0:T(8,128)(2,1)} %get-tuple-element.100), channel_id=1, source_target_pairs={{0,1},{1,0},{2,3},{3,2},{4,5},{5,4},{6,7},{7,6},{8,9},{9,8},{10,11... | collective-permute-start | bytes 1572872 | tf_op jit(solution)/shard_map/ppermute | solution.py:17
  83.1 16.6 %collective-permute-start.16 = (bf16[512,512]{1,0:T(8,128)(2,1)S(1)}, bf16[512,512]{1,0:T(8,128)(2,1)S(1)}, u32[]{:S(2)}, u32[]{:S(2)}) collective-permute-start(bf16[512,512]{1,0:T(8,128)(2,1)S(1)} %get-tuple-element.107), channel_id=1, source_target_pairs={{0,1},{1,0},{2,3},{3,2},{4,5},{5,4},{6,7},{7,6},{8,9},{9,8},{10,11... | collective-permute-start | bytes 1572872 | tf_op jit(solution)/shard_map/ppermute | solution.py:17
  83.2 16.6 %collective-permute-start.17 = (bf16[512,512]{1,0:T(8,128)(2,1)S(1)}, bf16[512,512]{1,0:T(8,128)(2,1)S(1)}, u32[]{:S(2)}, u32[]{:S(2)}) collective-permute-start(bf16[512,512]{1,0:T(8,128)(2,1)S(1)} %get-tuple-element.108), channel_id=1, source_target_pairs={{0,1},{1,0},{2,3},{3,2},{4,5},{5,4},{6,7},{7,6},{8,9},{9,8},{10,11... | collective-permute-start | bytes 1572872 | tf_op jit(solution)/shard_map/ppermute | solution.py:17
  92.0 13.3 %collective-permute-start.18 = (bf16[512,256]{1,0:T(8,128)(2,1)S(1)}, bf16[512,256]{1,0:T(8,128)(2,1)S(1)}, u32[]{:S(2)}, u32[]{:S(2)}) collective-permute-start(bf16[512,256]{1,0:T(8,128)(2,1)S(1)} %get-tuple-element.112), channel_id=1, source_target_pairs={{0,2},{1,3},{2,0},{3,1},{4,6},{5,7},{6,4},{7,5},{8,10},{9,11},{10,... | collective-permute-start | bytes 786440 | tf_op jit(solution)/shard_map/ppermute | solution.py:17
  92.5 16.6 %collective-permute-start.19 = (bf16[512,256]{1,0:T(8,128)(2,1)S(1)}, bf16[512,256]{1,0:T(8,128)(2,1)S(1)}, u32[]{:S(2)}, u32[]{:S(2)}) collective-permute-start(bf16[512,256]{1,0:T(8,128)(2,1)S(1)} %get-tuple-element.113), channel_id=1, source_target_pairs={{0,2},{1,3},{2,0},{3,1},{4,6},{5,7},{6,4},{7,5},{8,10},{9,11},{10,... | collective-permute-start | bytes 786440 | tf_op jit(solution)/shard_map/ppermute | solution.py:17
  112.3 19.5 %collective-permute-start.24 = (bf16[512,512]{1,0:T(8,128)(2,1)}, bf16[512,512]{1,0:T(8,128)(2,1)S(1)}, u32[]{:S(2)}, u32[]{:S(2)}) collective-permute-start(bf16[512,512]{1,0:T(8,128)(2,1)} %copy-done.7), channel_id=1, source_target_pairs={{0,1},{1,0},{2,3},{3,2},{4,5},{5,4},{6,7},{7,6},{8,9},{9,8},{10,11... | collective-permute-start | bytes 1572872 | tf_op jit(solution)/shard_map/ppermute | solution.py:17
  112.9 19.0 %collective-permute-start.25 = (bf16[512,512]{1,0:T(8,128)(2,1)}, bf16[512,512]{1,0:T(8,128)(2,1)S(1)}, u32[]{:S(2)}, u32[]{:S(2)}) collective-permute-start(bf16[512,512]{1,0:T(8,128)(2,1)} %copy-done.5), channel_id=1, source_target_pairs={{0,1},{1,0},{2,3},{3,2},{4,5},{5,4},{6,7},{7,6},{8,9},{9,8},{10,11... | collective-permute-start | bytes 1572872 | tf_op jit(solution)/shard_map/ppermute | solution.py:17
  113.0 26.1 %collective-permute-start.26 = (bf16[512,256]{1,0:T(8,128)(2,1)}, bf16[512,256]{1,0:T(8,128)(2,1)S(1)}, u32[]{:S(2)}, u32[]{:S(2)}) collective-permute-start(bf16[512,256]{1,0:T(8,128)(2,1)} %copy-done.10), channel_id=1, source_target_pairs={{0,2},{1,3},{2,0},{3,1},{4,6},{5,7},{6,4},{7,5},{8,10},{9,11},{10,... | collective-permute-start | bytes 786440 | tf_op jit(solution)/shard_map/ppermute | solution.py:17
  117.1 22.0 %collective-permute-start.27 = (bf16[512,256]{1,0:T(8,128)(2,1)S(1)}, bf16[512,256]{1,0:T(8,128)(2,1)S(1)}, u32[]{:S(2)}, u32[]{:S(2)}) collective-permute-start(bf16[512,256]{1,0:T(8,128)(2,1)S(1)} %get-tuple-element.121), channel_id=1, source_target_pairs={{0,2},{1,3},{2,0},{3,1},{4,6},{5,7},{6,4},{7,5},{8,10},{9,11},{10,... | collective-permute-start | bytes 786440 | tf_op jit(solution)/shard_map/ppermute | solution.py:17
  120.7 19.1 %collective-permute-start.21 = (bf16[512,512]{1,0:T(8,128)(2,1)S(1)}, bf16[512,512]{1,0:T(8,128)(2,1)S(1)}, u32[]{:S(2)}, u32[]{:S(2)}) collective-permute-start(bf16[512,512]{1,0:T(8,128)(2,1)S(1)} %pad_maximum_fusion.8), channel_id=1, source_target_pairs={{0,1},{1,0},{2,3},{3,2},{4,5},{5,4},{6,7},{7,6},{8,9},{9,8},{10,11... | collective-permute-start | bytes 1572872 | tf_op jit(solution)/shard_map/ppermute | solution.py:17
  136.9 30.5 %collective-permute-start.32 = (bf16[512,256]{1,0:T(8,128)(2,1)S(1)}, bf16[512,256]{1,0:T(8,128)(2,1)S(1)}, u32[]{:S(2)}, u32[]{:S(2)}) collective-permute-start(bf16[512,256]{1,0:T(8,128)(2,1)S(1)} %get-tuple-element.131), channel_id=1, source_target_pairs={{0,2},{1,3},{2,0},{3,1},{4,6},{5,7},{6,4},{7,5},{8,10},{9,11},{10,... | collective-permute-start | bytes 786440 | tf_op jit(solution)/shard_map/ppermute | solution.py:17
  137.0 30.7 %collective-permute-start.33 = (bf16[512,256]{1,0:T(8,128)(2,1)S(1)}, bf16[512,256]{1,0:T(8,128)(2,1)S(1)}, u32[]{:S(2)}, u32[]{:S(2)}) collective-permute-start(bf16[512,256]{1,0:T(8,128)(2,1)S(1)} %get-tuple-element.132), channel_id=1, source_target_pairs={{0,2},{1,3},{2,0},{3,1},{4,6},{5,7},{6,4},{7,5},{8,10},{9,11},{10,... | collective-permute-start | bytes 786440 | tf_op jit(solution)/shard_map/ppermute | solution.py:17
  139.0 22.9 %collective-permute-start.28 = (bf16[512,512]{1,0:T(8,128)(2,1)S(1)}, bf16[512,512]{1,0:T(8,128)(2,1)S(1)}, u32[]{:S(2)}, u32[]{:S(2)}) collective-permute-start(bf16[512,512]{1,0:T(8,128)(2,1)S(1)} %get-tuple-element.128), channel_id=1, source_target_pairs={{0,1},{1,0},{2,3},{3,2},{4,5},{5,4},{6,7},{7,6},{8,9},{9,8},{10,11... | collective-permute-start | bytes 1572872 | tf_op jit(solution)/shard_map/ppermute | solution.py:17
  139.0 23.4 %collective-permute-start.29 = (bf16[512,512]{1,0:T(8,128)(2,1)S(1)}, bf16[512,512]{1,0:T(8,128)(2,1)S(1)}, u32[]{:S(2)}, u32[]{:S(2)}) collective-permute-start(bf16[512,512]{1,0:T(8,128)(2,1)S(1)} %get-tuple-element.129), channel_id=1, source_target_pairs={{0,1},{1,0},{2,3},{3,2},{4,5},{5,4},{6,7},{7,6},{8,9},{9,8},{10,11... | collective-permute-start | bytes 1572872 | tf_op jit(solution)/shard_map/ppermute | solution.py:17
  139.8 17.2 %collective-permute-start.30 = (bf16[512,256]{1,0:T(8,128)(2,1)S(1)}, bf16[512,256]{1,0:T(8,128)(2,1)S(1)}, u32[]{:S(2)}, u32[]{:S(2)}) collective-permute-start(bf16[512,256]{1,0:T(8,128)(2,1)S(1)} %multiply_convert_fusion.6), channel_id=1, source_target_pairs={{0,2},{1,3},{2,0},{3,1},{4,6},{5,7},{6,4},{7,5},{8,10},{9,11},{10,... | collective-permute-start | bytes 786440 | tf_op jit(solution)/shard_map/ppermute | solution.py:17
  157.0 12.7 %collective-permute-start.31 = (bf16[512,512]{1,0:T(8,128)(2,1)S(1)}, bf16[512,512]{1,0:T(8,128)(2,1)S(1)}, u32[]{:S(2)}, u32[]{:S(2)}) collective-permute-start(bf16[512,512]{1,0:T(8,128)(2,1)S(1)} %pad_maximum_fusion.10), channel_id=1, source_target_pairs={{0,1},{1,0},{2,3},{3,2},{4,5},{5,4},{6,7},{7,6},{8,9},{9,8},{10,11... | collective-permute-start | bytes 1572872 | tf_op jit(solution)/shard_map/ppermute | solution.py:17
  161.9 20.0 %collective-permute-start.34 = (bf16[512,512]{1,0:T(8,128)(2,1)S(1)}, bf16[512,512]{1,0:T(8,128)(2,1)S(1)}, u32[]{:S(2)}, u32[]{:S(2)}) collective-permute-start(bf16[512,512]{1,0:T(8,128)(2,1)S(1)} %get-tuple-element.139), channel_id=1, source_target_pairs={{0,1},{1,0},{2,3},{3,2},{4,5},{5,4},{6,7},{7,6},{8,9},{9,8},{10,11... | collective-permute-start | bytes 1572872 | tf_op jit(solution)/shard_map/ppermute | solution.py:17
  162.4 19.4 %collective-permute-start.35 = (bf16[512,512]{1,0:T(8,128)(2,1)S(1)}, bf16[512,512]{1,0:T(8,128)(2,1)S(1)}, u32[]{:S(2)}, u32[]{:S(2)}) collective-permute-start(bf16[512,512]{1,0:T(8,128)(2,1)S(1)} %get-tuple-element.140), channel_id=1, source_target_pairs={{0,1},{1,0},{2,3},{3,2},{4,5},{5,4},{6,7},{7,6},{8,9},{9,8},{10,11... | collective-permute-start | bytes 1572872 | tf_op jit(solution)/shard_map/ppermute | solution.py:17
  167.4 19.4 %collective-permute-start.36 = (bf16[512,256]{1,0:T(8,128)(2,1)S(1)}, bf16[512,256]{1,0:T(8,128)(2,1)S(1)}, u32[]{:S(2)}, u32[]{:S(2)}) collective-permute-start(bf16[512,256]{1,0:T(8,128)(2,1)S(1)} %get-tuple-element.144), channel_id=1, source_target_pairs={{0,2},{1,3},{2,0},{3,1},{4,6},{5,7},{6,4},{7,5},{8,10},{9,11},{10,... | collective-permute-start | bytes 786440 | tf_op jit(solution)/shard_map/ppermute | solution.py:17
  167.7 19.0 %collective-permute-start.37 = (bf16[512,256]{1,0:T(8,128)(2,1)S(1)}, bf16[512,256]{1,0:T(8,128)(2,1)S(1)}, u32[]{:S(2)}, u32[]{:S(2)}) collective-permute-start(bf16[512,256]{1,0:T(8,128)(2,1)S(1)} %get-tuple-element.145), channel_id=1, source_target_pairs={{0,2},{1,3},{2,0},{3,1},{4,6},{5,7},{6,4},{7,5},{8,10},{9,11},{10,... | collective-permute-start | bytes 786440 | tf_op jit(solution)/shard_map/ppermute | solution.py:17
  169.7 19.8 %collective-permute-start.40 = (bf16[512,256]{1,0:T(8,128)(2,1)S(1)}, bf16[512,256]{1,0:T(8,128)(2,1)S(1)}, u32[]{:S(2)}, u32[]{:S(2)}) collective-permute-start(bf16[512,256]{1,0:T(8,128)(2,1)S(1)} %multiply_convert_fusion.5), channel_id=1, source_target_pairs={{0,2},{1,3},{2,0},{3,1},{4,6},{5,7},{6,4},{7,5},{8,10},{9,11},{10,... | collective-permute-start | bytes 786440 | tf_op jit(solution)/shard_map/ppermute | solution.py:17
  191.1 26.3 %collective-permute-start.44 = (bf16[512,256]{1,0:T(8,128)(2,1)}, bf16[512,256]{1,0:T(8,128)(2,1)S(1)}, u32[]{:S(2)}, u32[]{:S(2)}) collective-permute-start(bf16[512,256]{1,0:T(8,128)(2,1)} %copy-done.9), channel_id=1, source_target_pairs={{0,2},{1,3},{2,0},{3,1},{4,6},{5,7},{6,4},{7,5},{8,10},{9,11},{10,... | collective-permute-start | bytes 786440 | tf_op jit(solution)/shard_map/ppermute | solution.py:17
  191.4 26.0 %collective-permute-start.45 = (bf16[512,256]{1,0:T(8,128)(2,1)S(1)}, bf16[512,256]{1,0:T(8,128)(2,1)S(1)}, u32[]{:S(2)}, u32[]{:S(2)}) collective-permute-start(bf16[512,256]{1,0:T(8,128)(2,1)S(1)} %get-tuple-element.154), channel_id=1, source_target_pairs={{0,2},{1,3},{2,0},{3,1},{4,6},{5,7},{6,4},{7,5},{8,10},{9,11},{10,... | collective-permute-start | bytes 786440 | tf_op jit(solution)/shard_map/ppermute | solution.py:17
  193.2 17.2 %collective-permute-start.42 = (bf16[512,512]{1,0:T(8,128)(2,1)}, bf16[512,512]{1,0:T(8,128)(2,1)S(1)}, u32[]{:S(2)}, u32[]{:S(2)}) collective-permute-start(bf16[512,512]{1,0:T(8,128)(2,1)} %copy-done.8), channel_id=1, source_target_pairs={{0,1},{1,0},{2,3},{3,2},{4,5},{5,4},{6,7},{7,6},{8,9},{9,8},{10,11... | collective-permute-start | bytes 1572872 | tf_op jit(solution)/shard_map/ppermute | solution.py:17
  197.2 13.2 %collective-permute-start.43 = (bf16[512,512]{1,0:T(8,128)(2,1)}, bf16[512,512]{1,0:T(8,128)(2,1)S(1)}, u32[]{:S(2)}, u32[]{:S(2)}) collective-permute-start(bf16[512,512]{1,0:T(8,128)(2,1)} %copy-done.6), channel_id=1, source_target_pairs={{0,1},{1,0},{2,3},{3,2},{4,5},{5,4},{6,7},{7,6},{8,9},{9,8},{10,11... | collective-permute-start | bytes 1572872 | tf_op jit(solution)/shard_map/ppermute | solution.py:17
  198.4 19.8 %collective-permute-start.39 = (bf16[512,512]{1,0:T(8,128)(2,1)S(1)}, bf16[512,512]{1,0:T(8,128)(2,1)S(1)}, u32[]{:S(2)}, u32[]{:S(2)}) collective-permute-start(bf16[512,512]{1,0:T(8,128)(2,1)S(1)} %pad_maximum_fusion.11), channel_id=1, source_target_pairs={{0,1},{1,0},{2,3},{3,2},{4,5},{5,4},{6,7},{7,6},{8,9},{9,8},{10,11... | collective-permute-start | bytes 1572872 | tf_op jit(solution)/shard_map/ppermute | solution.py:17
  215.3 32.5 %collective-permute-start.50 = (bf16[512,256]{1,0:T(8,128)(2,1)S(1)}, bf16[512,256]{1,0:T(8,128)(2,1)S(1)}, u32[]{:S(2)}, u32[]{:S(2)}) collective-permute-start(bf16[512,256]{1,0:T(8,128)(2,1)S(1)} %get-tuple-element.164), channel_id=1, source_target_pairs={{0,2},{1,3},{2,0},{3,1},{4,6},{5,7},{6,4},{7,5},{8,10},{9,11},{10,... | collective-permute-start | bytes 786440 | tf_op jit(solution)/shard_map/ppermute | solution.py:17
  217.2 30.6 %collective-permute-start.51 = (bf16[512,256]{1,0:T(8,128)(2,1)S(1)}, bf16[512,256]{1,0:T(8,128)(2,1)S(1)}, u32[]{:S(2)}, u32[]{:S(2)}) collective-permute-start(bf16[512,256]{1,0:T(8,128)(2,1)S(1)} %get-tuple-element.165), channel_id=1, source_target_pairs={{0,2},{1,3},{2,0},{3,1},{4,6},{5,7},{6,4},{7,5},{8,10},{9,11},{10,... | collective-permute-start | bytes 786440 | tf_op jit(solution)/shard_map/ppermute | solution.py:17
  217.4 23.4 %collective-permute-start.46 = (bf16[512,512]{1,0:T(8,128)(2,1)S(1)}, bf16[512,512]{1,0:T(8,128)(2,1)S(1)}, u32[]{:S(2)}, u32[]{:S(2)}) collective-permute-start(bf16[512,512]{1,0:T(8,128)(2,1)S(1)} %get-tuple-element.161), channel_id=1, source_target_pairs={{0,1},{1,0},{2,3},{3,2},{4,5},{5,4},{6,7},{7,6},{8,9},{9,8},{10,11... | collective-permute-start | bytes 1572872 | tf_op jit(solution)/shard_map/ppermute | solution.py:17
  217.5 23.3 %collective-permute-start.47 = (bf16[512,512]{1,0:T(8,128)(2,1)S(1)}, bf16[512,512]{1,0:T(8,128)(2,1)S(1)}, u32[]{:S(2)}, u32[]{:S(2)}) collective-permute-start(bf16[512,512]{1,0:T(8,128)(2,1)S(1)} %get-tuple-element.162), channel_id=1, source_target_pairs={{0,1},{1,0},{2,3},{3,2},{4,5},{5,4},{6,7},{7,6},{8,9},{9,8},{10,11... | collective-permute-start | bytes 1572872 | tf_op jit(solution)/shard_map/ppermute | solution.py:17
  218.2 17.2 %collective-permute-start.48 = (bf16[512,256]{1,0:T(8,128)(2,1)S(1)}, bf16[512,256]{1,0:T(8,128)(2,1)S(1)}, u32[]{:S(2)}, u32[]{:S(2)}) collective-permute-start(bf16[512,256]{1,0:T(8,128)(2,1)S(1)} %multiply_convert_fusion.3), channel_id=1, source_target_pairs={{0,2},{1,3},{2,0},{3,1},{4,6},{5,7},{6,4},{7,5},{8,10},{9,11},{10,... | collective-permute-start | bytes 786440 | tf_op jit(solution)/shard_map/ppermute | solution.py:17
  235.5 14.3 %collective-permute-start.49 = (bf16[512,512]{1,0:T(8,128)(2,1)S(1)}, bf16[512,512]{1,0:T(8,128)(2,1)S(1)}, u32[]{:S(2)}, u32[]{:S(2)}) collective-permute-start(bf16[512,512]{1,0:T(8,128)(2,1)S(1)} %pad_maximum_fusion.13), channel_id=1, source_target_pairs={{0,1},{1,0},{2,3},{3,2},{4,5},{5,4},{6,7},{7,6},{8,9},{9,8},{10,11... | collective-permute-start | bytes 1572872 | tf_op jit(solution)/shard_map/ppermute | solution.py:17
  247.5 13.0 %collective-permute-start.53 = (bf16[512,256]{1,0:T(8,128)(2,1)S(1)}, bf16[512,256]{1,0:T(8,128)(2,1)S(1)}, u32[]{:S(2)}, u32[]{:S(2)}) collective-permute-start(bf16[512,256]{1,0:T(8,128)(2,1)S(1)} %get-tuple-element.175), channel_id=1, source_target_pairs={{0,2},{1,3},{2,0},{3,1},{4,6},{5,7},{6,4},{7,5},{8,10},{9,11},{10,... | collective-permute-start | bytes 786440 | tf_op jit(solution)/shard_map/ppermute | solution.py:17
  248.0 18.1 %collective-permute-start.56 = (bf16[512,256]{1,0:T(8,128)(2,1)S(1)}, bf16[512,256]{1,0:T(8,128)(2,1)S(1)}, u32[]{:S(2)}, u32[]{:S(2)}) collective-permute-start(bf16[512,256]{1,0:T(8,128)(2,1)S(1)} %multiply_convert_fusion.2), channel_id=1, source_target_pairs={{0,2},{1,3},{2,0},{3,1},{4,6},{5,7},{6,4},{7,5},{8,10},{9,11},{10,... | collective-permute-start | bytes 786440 | tf_op jit(solution)/shard_map/ppermute | solution.py:17
  286.1 12.6 %collective-permute-start.58 = (bf16[512,512]{1,0:T(8,128)(2,1)S(1)}, bf16[512,512]{1,0:T(8,128)(2,1)S(1)}, u32[]{:S(2)}, u32[]{:S(2)}) collective-permute-start(bf16[512,512]{1,0:T(8,128)(2,1)S(1)} %get-tuple-element.187), channel_id=1, source_target_pairs={{0,4},{1,5},{2,6},{3,7},{16,20},{17,21},{18,22},{19,23}} | collective-permute-start | bytes 1572872 | tf_op jit(solution)/shard_map/ppermute | solution.py:27
  287.6 17.0 %collective-permute-start.61 = (bf16[512,512]{1,0:T(8,128)(2,1)S(1)}, bf16[512,512]{1,0:T(8,128)(2,1)S(1)}, u32[]{:S(2)}, u32[]{:S(2)}) collective-permute-start(bf16[512,512]{1,0:T(8,128)(2,1)S(1)} %get-tuple-element.188), channel_id=1, source_target_pairs={{12,8},{13,9},{14,10},{15,11},{28,24},{29,25},{30,26},{31,27}} | collective-permute-start | bytes 1572872 | tf_op jit(solution)/shard_map/ppermute | solution.py:27
  300.1 14.7 %collective-permute-start.59 = (bf16[512,512]{1,0:T(8,128)(2,1)S(1)}, bf16[512,512]{1,0:T(8,128)(2,1)S(1)}, u32[]{:S(2)}, u32[]{:S(2)}) collective-permute-start(bf16[512,512]{1,0:T(8,128)(2,1)S(1)} %add_convert_fusion.4), channel_id=1, source_target_pairs={{0,4},{1,5},{2,6},{3,7},{4,8},{5,9},{6,10},{7,11},{16,20},{17,21},... | collective-permute-start | bytes 1572872 | tf_op jit(solution)/shard_map/ppermute | solution.py:27
  317.5 14.4 %collective-permute-start.60 = (bf16[512,512]{1,0:T(8,128)(2,1)S(1)}, bf16[512,512]{1,0:T(8,128)(2,1)S(1)}, u32[]{:S(2)}, u32[]{:S(2)}) collective-permute-start(bf16[512,512]{1,0:T(8,128)(2,1)S(1)} %get-tuple-element.185), channel_id=1, source_target_pairs={{0,4},{1,5},{2,6},{3,7},{4,8},{5,9},{6,10},{7,11},{8,12},{9,13},{1... | collective-permute-start | bytes 1572872 | tf_op jit(solution)/shard_map/ppermute | solution.py:27
  324.0 21.6 %collective-permute-start.63 = (bf16[512,512]{1,0:T(8,128)(2,1)S(1)}, bf16[512,512]{1,0:T(8,128)(2,1)S(1)}, u32[]{:S(2)}, u32[]{:S(2)}) collective-permute-start(bf16[512,512]{1,0:T(8,128)(2,1)S(1)} %add_convert_fusion.1), channel_id=1, source_target_pairs={{4,0},{5,1},{6,2},{7,3},{8,4},{9,5},{10,6},{11,7},{12,8},{13,9},{1... | collective-permute-start | bytes 1572872 | tf_op jit(solution)/shard_map/ppermute | solution.py:27
  (37 other events, 285.3 us)
